TPU v7x, 32 devices: a whole 2x2x4 slice. The times are simulated.
32 devices in a mesh: dp: 8 (over y, x, core), tensor: 4 (over z).
Axes of the slice: x: 2, y: 2, z: 4, core: 2. Of those that a mesh axis runs over, the one named last changes fastest.
Arguments:
- inputs: bfloat16 [32, 1024, 768], P('dp', 'tensor'), may hold values from -6 to 6
- doc_ids: int32 [32, 1024], P('dp'), may hold values from 0 to 2, as said below
- ln1_gain: float32 [768], replicated, may hold values from 0.1 to 1.9
- ln1_bias: float32 [768], replicated, may hold values from -1.5 to 1.5
- w_qkv: bfloat16 [768, 3, 768], P(None, None, 'tensor'), may hold values from -0.21875 to 0.21875
- b_qv: float32 [2, 768], P(None, 'tensor'), may hold values from -1.5 to 1.5
- w_out: bfloat16 [768, 768], P('tensor'), may hold values from -1.75 to 1.75
- out_bias: float32 [768], replicated, may hold values from -1.5 to 1.5
- ln2_gain: float32 [768], replicated, may hold values from 0.1 to 1.9
- ln2_bias: float32 [768], replicated, may hold values from -1.5 to 1.5
- w_up: bfloat16 [768, 3072], P(None, 'tensor'), may hold values from -0.21875 to 0.21875
- b_up: float32 [3072], P('tensor'), may hold values from -1.5 to 1.5
- w_down: bfloat16 [3072, 768], P('tensor'), may hold values from -0.15625 to 0.15625
- down_bias: float32 [768], replicated, may hold values from -1.5 to 1.5
- cotangent: bfloat16 [32, 1024, 768], P('dp', 'tensor'), may hold values from -6 to 6
Outputs:
- block_out: bfloat16 [32, 1024, 768], P('dp', 'tensor')
- grad_inputs: bfloat16 [32, 1024, 768], P('dp', 'tensor')
- grad_ln1_gain: float32 [768], P(('dp', 'tensor'))
- grad_ln1_bias: float32 [768], P(('dp', 'tensor'))
- grad_w_qkv: float32 [768, 3, 768], P('dp', None, 'tensor')
- grad_b_qv: float32 [2, 768], P(None, ('tensor', 'dp'))
- grad_w_out: float32 [768, 768], P('tensor', 'dp')
- grad_out_bias: float32 [768], P(('dp', 'tensor'))
- grad_ln2_gain: float32 [768], P(('dp', 'tensor'))
- grad_ln2_bias: float32 [768], P(('dp', 'tensor'))
- grad_w_up: float32 [768, 3072], P('dp', 'tensor')
- grad_b_up: float32 [3072], P(('tensor', 'dp'))
- grad_w_down: float32 [3072, 768], P('tensor', 'dp')
- grad_down_bias: float32 [768], P(('dp', 'tensor'))
Inputs may be any that keep to these rules, and one draw needn't show every extreme that they name: `doc_ids`: along every row the ids start at 0, never fall, and a document ends where the id changes; every row holds one document of exactly 769 tokens, its longest.
All inputs are finite; a program needn't handle non-finite values.
Results may differ from a plain program's by a relative error of at most 0.02.
Values may be sent and summed in bfloat16 or wider, within the bound.
No kernel may reach another device: no remote copies, remote signals or barrier semaphores. Data moves between devices by JAX's collectives and lax.ppermute only.
A program may use at most 320 MiB of HBM per device.

v0:
```python
import jax
import jax.numpy as jnp
from jax import lax
from jax.sharding import PartitionSpec as P


def norm_rows(value_in, gain, bias):
    mean_row = jnp.mean(value_in, axis=-1, keepdims=True)
    centred = value_in - mean_row
    variance = jnp.mean(centred * centred, axis=-1, keepdims=True)
    return centred * lax.rsqrt(variance + 1e-05) * gain + bias


def gelu_tanh(pre_act):
    return jax.nn.gelu(pre_act, approximate=True)


def block_scores(query_blk, key_used, doc_rows, first, block, key_count):
    scores = (
        jnp.einsum("rqhe,rkhe->rhqk", query_blk, key_used, preferred_element_type=jnp.float32)
        * 0.125
    )
    place_q = first + jnp.arange(block)
    place_k = jnp.arange(key_count)
    docs_q = doc_rows[:, first : first + block]
    allowed = (docs_q[:, :, None] == doc_rows[:, None, :]) & (place_q[:, None] >= place_k[None, :])[
        None
    ]
    return jnp.where(allowed[:, None], scores, -1e30)


def attend_forward(query_h, key_h, value_h, doc_rows):
    seq_len = query_h.shape[1]
    block = min(512, seq_len)
    outputs = []
    logsums = []
    for first in range(0, seq_len, block):
        scores = block_scores(
            query_h[:, first : first + block], key_h, doc_rows, first, block, seq_len
        )
        top_row = jnp.max(scores, axis=-1, keepdims=True)
        expo = jnp.exp(scores - top_row)
        total = jnp.sum(expo, axis=-1, keepdims=True)
        probs_low = (expo / total).astype(jnp.bfloat16)
        outputs.append(
            jnp.einsum("rhqk,rkhe->rqhe", probs_low, value_h, preferred_element_type=jnp.float32)
        )
        logsums.append(top_row + jnp.log(total))
    return (jnp.concatenate(outputs, axis=1), logsums)


def attend_backward(query_h, key_h, value_h, doc_rows, logsums, grad_out):
    seq_len = query_h.shape[1]
    block = min(512, seq_len)
    grad_queries = []
    grad_keys = jnp.zeros(key_h.shape, jnp.float32)
    grad_values = jnp.zeros(value_h.shape, jnp.float32)
    for index_blk, first in enumerate(range(0, seq_len, block)):
        query_blk = query_h[:, first : first + block]
        grad_blk = grad_out[:, first : first + block]
        scores = block_scores(query_blk, key_h, doc_rows, first, block, seq_len)
        probs = jnp.exp(scores - logsums[index_blk])
        probs_low = probs.astype(jnp.bfloat16)
        grad_probs = jnp.einsum(
            "rqhe,rkhe->rhqk", grad_blk, value_h, preferred_element_type=jnp.float32
        )
        delta = jnp.sum(probs * grad_probs, axis=-1, keepdims=True)
        grad_scores = (probs * (grad_probs - delta)).astype(jnp.bfloat16)
        grad_queries.append(
            jnp.einsum("rhqk,rkhe->rqhe", grad_scores, key_h, preferred_element_type=jnp.float32)
            * 0.125
        )
        grad_keys = grad_keys.at[:, :seq_len].add(
            jnp.einsum(
                "rhqk,rqhe->rkhe", grad_scores, query_blk, preferred_element_type=jnp.float32
            )
            * 0.125
        )
        grad_values = grad_values.at[:, :seq_len].add(
            jnp.einsum("rhqk,rqhe->rkhe", probs_low, grad_blk, preferred_element_type=jnp.float32)
        )
    return (jnp.concatenate(grad_queries, axis=1), grad_keys, grad_values)


def local(
    inputs,
    doc_ids,
    ln1_gain,
    ln1_bias,
    w_qkv,
    b_qv,
    w_out,
    out_bias,
    ln2_gain,
    ln2_bias,
    w_up,
    b_up,
    w_down,
    down_bias,
    cotangent,
):
    n_rows = inputs.shape[0]
    head_count = w_qkv.shape[2] // 64
    inputs_f = inputs.astype(jnp.float32)
    normed_one = norm_rows(inputs_f, ln1_gain, ln1_bias).astype(jnp.bfloat16)
    rows_one = lax.all_gather(normed_one, "tensor", axis=1, tiled=True)
    seq_len = rows_one.shape[1]
    projected = jnp.einsum("rld,dcm->rlcm", rows_one, w_qkv, preferred_element_type=jnp.float32)
    queries = (projected[:, :, 0] + b_qv[0]).astype(jnp.bfloat16)
    keyed = projected[:, :, 1].astype(jnp.bfloat16)
    valued = (projected[:, :, 2] + b_qv[1]).astype(jnp.bfloat16)

    def by_head(tensor_in):
        return tensor_in.reshape(n_rows, seq_len, head_count, 64)

    attended, logsums = attend_forward(by_head(queries), by_head(keyed), by_head(valued), doc_ids)
    attended = attended.reshape(n_rows, seq_len, -1).astype(jnp.bfloat16)
    attn_part = jnp.einsum("rlm,md->rld", attended, w_out, preferred_element_type=jnp.float32)
    mixed = (
        inputs_f
        + lax.psum_scatter(
            attn_part.astype(jnp.bfloat16), "tensor", scatter_dimension=1, tiled=True
        ).astype(jnp.float32)
        + out_bias
    )
    normed_two = norm_rows(mixed, ln2_gain, ln2_bias).astype(jnp.bfloat16)
    rows_two = lax.all_gather(normed_two, "tensor", axis=1, tiled=True)
    pre_act = jnp.einsum("rld,df->rlf", rows_two, w_up, preferred_element_type=jnp.float32) + b_up
    activated = gelu_tanh(pre_act).astype(jnp.bfloat16)
    down_part = jnp.einsum("rlf,fd->rld", activated, w_down, preferred_element_type=jnp.float32)
    block_out = (
        mixed
        + lax.psum_scatter(
            down_part.astype(jnp.bfloat16), "tensor", scatter_dimension=1, tiled=True
        ).astype(jnp.float32)
        + down_bias
    ).astype(jnp.bfloat16)
    grad_top = cotangent.astype(jnp.float32)
    grad_down_bias = jnp.sum(grad_top, axis=(0, 1))
    cot_rows = lax.all_gather(cotangent, "tensor", axis=1, tiled=True)
    grad_w_down = jnp.einsum("rlf,rld->fd", activated, cot_rows, preferred_element_type=jnp.float32)
    grad_act = jnp.einsum("rld,fd->rlf", cot_rows, w_down, preferred_element_type=jnp.float32)
    gelu_value, gelu_back = jax.vjp(gelu_tanh, pre_act)
    grad_pre = gelu_back(grad_act)[0].astype(jnp.bfloat16)
    grad_b_up = jnp.sum(grad_pre.astype(jnp.float32), axis=(0, 1))
    grad_w_up = jnp.einsum("rld,rlf->df", rows_two, grad_pre, preferred_element_type=jnp.float32)
    norm_two_part = jnp.einsum("rlf,df->rld", grad_pre, w_up, preferred_element_type=jnp.float32)
    grad_normed_two = lax.psum_scatter(
        norm_two_part.astype(jnp.bfloat16), "tensor", scatter_dimension=1, tiled=True
    ).astype(jnp.float32)
    norm_value, norm_two_back = jax.vjp(norm_rows, mixed, ln2_gain, ln2_bias)
    grad_mixed_ln, grad_ln2_gain, grad_ln2_bias = norm_two_back(grad_normed_two)
    grad_mixed = grad_top + grad_mixed_ln
    grad_out_bias = jnp.sum(grad_mixed, axis=(0, 1))
    grad_mixed_low = grad_mixed.astype(jnp.bfloat16)
    resid_rows = lax.all_gather(grad_mixed_low, "tensor", axis=1, tiled=True)
    grad_w_out = jnp.einsum("rlm,rld->md", attended, resid_rows, preferred_element_type=jnp.float32)
    grad_attended = jnp.einsum(
        "rld,md->rlm", resid_rows, w_out, preferred_element_type=jnp.float32
    ).astype(jnp.bfloat16)
    grad_q, grad_k, grad_v = attend_backward(
        by_head(queries), by_head(keyed), by_head(valued), doc_ids, logsums, by_head(grad_attended)
    )
    grad_proj = jnp.stack(
        [
            grad_q.reshape(n_rows, seq_len, -1),
            grad_k.reshape(n_rows, seq_len, -1),
            grad_v.reshape(n_rows, seq_len, -1),
        ],
        axis=2,
    ).astype(jnp.bfloat16)
    grad_w_qkv = jnp.einsum(
        "rld,rlcm->dcm", rows_one, grad_proj, preferred_element_type=jnp.float32
    )
    grad_b_qv = jnp.sum(grad_proj[:, :, 0::2].astype(jnp.float32), axis=(0, 1))
    norm_one_part = jnp.einsum(
        "rlcm,dcm->rld", grad_proj, w_qkv, preferred_element_type=jnp.float32
    )
    shares = (
        lax.psum_scatter(grad_w_qkv, "dp", scatter_dimension=0, tiled=True),
        lax.psum_scatter(grad_b_qv, "dp", scatter_dimension=1, tiled=True),
        lax.psum_scatter(grad_w_out, "dp", scatter_dimension=1, tiled=True),
        lax.psum_scatter(grad_w_up, "dp", scatter_dimension=0, tiled=True),
        lax.psum_scatter(grad_b_up, "dp", scatter_dimension=0, tiled=True),
        lax.psum_scatter(grad_w_down, "dp", scatter_dimension=1, tiled=True),
    )
    share_w_qkv, share_b_qv, share_w_out, share_w_up, share_b_up, share_w_down = shares
    grad_normed_one = lax.psum_scatter(
        norm_one_part.astype(jnp.bfloat16), "tensor", scatter_dimension=1, tiled=True
    ).astype(jnp.float32)
    norm_first, norm_one_back = jax.vjp(norm_rows, inputs_f, ln1_gain, ln1_bias)
    grad_in_ln, grad_ln1_gain, grad_ln1_bias = norm_one_back(grad_normed_one)
    grad_inputs = (grad_mixed + grad_in_ln).astype(jnp.bfloat16)
    vector_shares = (
        lax.psum_scatter(grad_ln1_gain, ("dp", "tensor"), scatter_dimension=0, tiled=True),
        lax.psum_scatter(grad_ln1_bias, ("dp", "tensor"), scatter_dimension=0, tiled=True),
        lax.psum_scatter(grad_out_bias, ("dp", "tensor"), scatter_dimension=0, tiled=True),
        lax.psum_scatter(grad_ln2_gain, ("dp", "tensor"), scatter_dimension=0, tiled=True),
        lax.psum_scatter(grad_ln2_bias, ("dp", "tensor"), scatter_dimension=0, tiled=True),
        lax.psum_scatter(grad_down_bias, ("dp", "tensor"), scatter_dimension=0, tiled=True),
    )
    return (
        block_out,
        grad_inputs,
        vector_shares[0],
        vector_shares[1],
        share_w_qkv,
        share_b_qv,
        share_w_out,
        vector_shares[2],
        vector_shares[3],
        vector_shares[4],
        share_w_up,
        share_b_up,
        share_w_down,
        vector_shares[5],
    )


def solution(mesh):
    return jax.shard_map(
        local,
        mesh=mesh,
        in_specs=(
            P("dp", "tensor", None),
            P("dp", None),
            P(),
            P(),
            P(None, None, "tensor"),
            P(None, "tensor"),
            P("tensor", None),
            P(),
            P(),
            P(),
            P(None, "tensor"),
            P("tensor"),
            P("tensor", None),
            P(),
            P("dp", "tensor", None),
        ),
        out_specs=(
            P("dp", "tensor", None),
            P("dp", "tensor", None),
            P(("dp", "tensor")),
            P(("dp", "tensor")),
            P("dp", None, "tensor"),
            P(None, ("tensor", "dp")),
            P("tensor", "dp"),
            P(("dp", "tensor")),
            P(("dp", "tensor")),
            P(("dp", "tensor")),
            P("dp", "tensor"),
            P(("tensor", "dp")),
            P("tensor", "dp"),
            P(("dp", "tensor")),
        ),
        check_vma=False,
    )
```

profile of v0, /device:TPU:0, one launch (start us, length us, event | category | flops | bytes accessed | tf_op | source)
XLA Modules:
  0.0 1342.2 jit_solution(6178811140442511821)
XLA Ops:
  14.9 4.4 compare_and_fusion.1
  19.3 113.1 %all-gather.5.cloned.1.call-done = bf16[4,1024,768]{2,1,0:T(8,128)(2,1)} async-done(((bf16[4,256,768]{2,1,0:T(8,128)(2,1)}), bf16[4,1024,768]{2,1,0:T(8,128)(2,1)}) %all-gather.5.cloned.1.call-update) | async-done | bytes 6291472 | tf_op jit(solution)/shard_map/all_gather | solution.py:106
  132.4 6.2 fusion.21
  141.4 10.8 fusion.80
  152.3 10.8 fusion.81
  163.6 11.5 fusion.1
  175.2 10.4 fusion.53
  185.6 11.2 fusion
  196.8 10.4 fusion.52
  208.6 4.5 convolution_convert_fusion
  213.1 109.0 %reduce-scatter.12.cloned.1.call-done = bf16[4,256,768]{2,1,0:T(8,128)(2,1)} async-done(((bf16[4,1024,768]{2,1,0:T(8,128)(2,1)}), bf16[4,256,768]{2,1,0:T(8,128)(2,1)}) %reduce-scatter.12.cloned.1.call-update) | async-done | bytes 1572880 | tf_op jit(solution)/shard_map/reduce_scatter | solution.py:121
  327.9 115.4 %all-gather.7.cloned.1.call-done = bf16[4,1024,768]{2,1,0:T(8,128)(2,1)} async-done(((bf16[4,256,768]{2,1,0:T(8,128)(2,1)}), bf16[4,1024,768]{2,1,0:T(8,128)(2,1)}) %all-gather.7.cloned.1.call-update) | async-done | bytes 6291472 | tf_op jit(solution)/shard_map/all_gather | solution.py:127
  443.3 10.6 fusion.57
  453.9 104.4 %all-gather.9.cloned.1.call-done = bf16[4,1024,768]{2,1,0:T(8,128)(2,1)} async-done(((bf16[4,256,768]{2,1,0:T(8,128)(2,1)}), bf16[4,1024,768]{2,1,0:T(8,128)(2,1)}) %all-gather.9.cloned.1.call-update) | async-done | bytes 6291472 | tf_op jit(solution)/shard_map/all_gather | solution.py:140
  558.3 17.0 %convert_reduce_fusion = (f32[768]{0:T(1024)}, bf16[4,1024,768]{2,1,0:T(8,128)(2,1)S(1)}) fusion(f32[4,1024,768]{2,1,0:T(8,128)} %fusion.57, f32[768]{0:T(1024)S(1)} %copy-done.60, bf16[4,1024,768]{2,1,0:T(8,128)(2,1)} %all-gather.9.cloned.1.call-done, bf16[768,768]{1,0:T(8,128)(2,1)S(1)} %copy-done), kind=kOutput, calls=%fused_computation.28 | convolution fusion | flops 4904188928 | bytes 26351616 | tf_op jit(solution)/shard_map/rld,fd->rlf/dot_general | solution.py:142
  575.3 2.7 copy-done.62
  578.0 7.1 convolution_convert_fusion.1
  585.2 109.1 %reduce-scatter.16.cloned.1.call-done = bf16[4,256,768]{2,1,0:T(8,128)(2,1)} async-done(((bf16[4,1024,768]{2,1,0:T(8,128)(2,1)}), bf16[4,256,768]{2,1,0:T(8,128)(2,1)}) %reduce-scatter.16.cloned.1.call-update) | async-done | bytes 1572880 | tf_op jit(solution)/shard_map/reduce_scatter | solution.py:148
  694.3 4.0 convert_reduce_fusion.3
  700.2 2.6 fusion.77
  703.0 115.9 %all-gather.11.cloned.1.call-done = bf16[4,1024,768]{2,1,0:T(8,128)(2,1)} async-done(((bf16[4,256,768]{2,1,0:T(8,128)(2,1)}), bf16[4,1024,768]{2,1,0:T(8,128)(2,1)}) %all-gather.11.cloned.1.call-update) | async-done | bytes 6291472 | tf_op jit(solution)/shard_map/all_gather | solution.py:156
  818.9 5.0 convolution_convert_fusion.3
  825.0 12.1 fusion.11
  837.1 16.4 %multiply_reduce_fusion = (f32[4,3,512]{2,1,0:T(4,128)}, f32[4,3,512,1024]{3,2,1,0:T(8,128)}) fusion(f32[4,3,512,1024]{3,2,1,0:T(8,128)} %get-tuple-element.123, f32[4,3,512]{2,1,0:T(4,128)S(1)} %log_add_fusion, bf16[4,1024,3,64]{1,3,2,0:T(8,128)(2,1)S(1)} %copy-done.12, bf16[4,1024,3,64]{1,3,2,0:T(8,128)(2,1)} %bitcast.121), kind=kOutput, calls=%fused_computation.1 | convolution fusion | flops 824174592 | bytes 52740096 | tf_op jit(solution)/shard_map/rqhe,rkhe->rhqk/dot_general | solution.py:64
  853.5 15.8 %multiply_reduce_fusion.1 = (f32[4,3,512]{2,1,0:T(4,128)S(1)}, f32[4,3,512,1024]{3,2,1,0:T(8,128)}) fusion(f32[4,3,512,1024]{3,2,1,0:T(8,128)} %get-tuple-element.125, f32[4,3,512]{2,1,0:T(4,128)S(1)} %log_add_fusion.1, bf16[4,1024,3,64]{1,3,2,0:T(8,128)(2,1)S(1)} %copy-done.12, bf16[4,1024,3,64]{1,3,2,0:T(8,128)(2,1)} %bitcast.122), kind=kOutput, calls=%fused_computation.4 | convolution fusion | flops 824174592 | bytes 52740096 | tf_op jit(solution)/shard_map/rqhe,rkhe->rhqk/dot_general | solution.py:64
  869.3 21.8 %multiply_convert_fusion.1 = bf16[4,3,512,1024]{3,2,1,0:T(8,128)(2,1)} fusion(f32[4,3,512,1024]{3,2,1,0:T(8,128)} %get-tuple-element.127, f32[4,3,512,1024]{3,2,1,0:T(8,128)} %get-tuple-element.125, f32[4,3,512]{2,1,0:T(4,128)S(1)} %get-tuple-element.126, f32[4,3,512]{2,1,0:T(4,128)S(1)} %log_add_fusion.1), kind=kLoop, calls=%fused_computation.3 | loop fusion | flops 25165824 | bytes 62963712 | tf_op jit(solution)/shard_map/convert_element_type | solution.py:68
  891.1 8.7 fusion.50
  899.8 8.7 fusion.69
  908.5 3.5 convolution_bitcast_fusion.2
  912.0 12.6 add_convert_fusion.1
  924.7 22.2 %multiply_convert_fusion = bf16[4,3,512,1024]{3,2,1,0:T(8,128)(2,1)} fusion(f32[4,3,512,1024]{3,2,1,0:T(8,128)} %get-tuple-element.129, f32[4,3,512,1024]{3,2,1,0:T(8,128)} %get-tuple-element.123, f32[4,3,512]{2,1,0:T(4,128)S(1)} %copy-done.40, f32[4,3,512]{2,1,0:T(4,128)S(1)} %copy-done.28), kind=kLoop, calls=%fused_computation | loop fusion | flops 25165824 | bytes 62963712 | tf_op jit(solution)/shard_map/convert_element_type | solution.py:68
  946.8 8.6 fusion.51
  955.5 6.9 multiply_convert_fusion.3
  964.2 7.2 bitcast_convert_fusion
  971.5 12.8 convolution_convert_fusion.2
  984.4 14.4 %convolution_bitcast_fusion = f32[768,768]{0,1:T(8,128)} fusion(bf16[4,1024,768]{2,1,0:T(8,128)(2,1)} %all-gather.9.cloned.1.call-done, f32[4,1024,768]{2,1,0:T(8,128)} %fusion.57, f32[768]{0:T(1024)S(1)} %copy-done.60), kind=kOutput, calls=%fused_computation.89 | convolution fusion | flops 4863295488 | bytes 21236736 | tf_op jit(solution)/shard_map/rlf,rld->fd/dot_general | solution.py:141
  1000.8 10.5 convolution_bitcast_fusion.1
  1011.3 10.2 fusion.42
  1021.5 3.8 pad_maximum_fusion
  1027.9 14.9 %all-reduce.9 = (f32[2,192]{1,0:T(2,128)S(1)}, f32[768]{0:T(1024)S(1)}) all-reduce(f32[2,192]{1,0:T(2,128)S(1)} %convert_reduce_fusion.1, f32[768]{0:T(1024)S(1)} %copy-done.55), channel_id=9, replica_groups=mesh['dp'=8,'tensor'=4] {'dp'}, use_global_device_ids=true, to_apply=%region_24.25.clone | all-reduce | flops 1152 | bytes 9216
  1045.7 34.8 %reduce-scatter.18.cloned.1.call-done = bf16[4,256,768]{2,1,0:T(8,128)(2,1)} async-done(((bf16[4,1024,768]{2,1,0:T(8,128)(2,1)}), bf16[4,256,768]{2,1,0:T(8,128)(2,1)}) %reduce-scatter.18.cloned.1.call-update) | async-done | bytes 1572880 | tf_op jit(solution)/shard_map/reduce_scatter | solution.py:188
  1083.0 5.5 fusion.37
  1088.5 46.9 %all-reduce.8 = (f32[768]{0:T(1024)S(1)}, f32[768]{0:T(1024)S(1)}, f32[768]{0:T(1024)S(1)}, f32[768]{0:T(1024)S(1)}, f32[768]{0:T(1024)S(1)}, /*index=5*/f32[768]{0:T(1024)S(1)}) all-reduce(f32[768]{0:T(1024)S(1)} %get-tuple-element.102, f32[768]{0:T(1024)S(1)} %get-tuple-element.103, ...), channel_id=6, replica_groups=mesh['dp'=8,'tensor'=4] {'dp','tensor'}, use_global_device_ids=true, to_apply=%region_19.20.clone | all-reduce | flops 4608 | bytes 36864
  1138.9 56.2 %reduce-scatter.14.cloned.1.call-done = bf16[4,256,768]{2,1,0:T(8,128)(2,1)} async-done(((bf16[4,1024,768]{2,1,0:T(8,128)(2,1)}), bf16[4,256,768]{2,1,0:T(8,128)(2,1)}) %reduce-scatter.14.cloned.1.call-update) | async-done | bytes 1572880 | tf_op jit(solution)/shard_map/reduce_scatter | solution.py:133
  1195.1 6.9 add_convert_fusion
  1202.0 39.9 %reduce-scatter.24.cloned.1.call-done = f32[768,96]{0,1:T(8,128)} async-done(((f32[768,768]{0,1:T(8,128)}), f32[768,96]{0,1:T(8,128)}) %reduce-scatter.24.cloned.1.call-update) | async-done | bytes 294928 | tf_op jit(solution)/shard_map/reduce_scatter | solution.py:185
  1241.9 46.8 %reduce-scatter.22.cloned.1.call-done = f32[96,768]{1,0:T(8,128)} async-done(((f32[768,768]{1,0:T(8,128)}), f32[96,768]{1,0:T(8,128)}) %reduce-scatter.22.cloned.1.call-update) | async-done | bytes 294928 | tf_op jit(solution)/shard_map/reduce_scatter | solution.py:183
  1288.7 46.3 %reduce-scatter.20.cloned.1.call-done = f32[96,3,192]{2,0,1:T(8,128)} async-done(((f32[768,3,192]{2,0,1:T(8,128)}), f32[96,3,192]{2,0,1:T(8,128)}) %reduce-scatter.20.cloned.1.call-update) | async-done | bytes 221200 | tf_op jit(solution)/shard_map/reduce_scatter | solution.py:180
  (196 shorter events, 35.4 us)
Async XLA Ops:
  7.2 551.2 %copy-start = (bf16[768,768]{1,0:T(8,128)(2,1)S(1)}, bf16[768,768]{1,0:T(8,128)(2,1)}, u32[]{:S(2)}) copy-start(bf16[768,768]{1,0:T(8,128)(2,1)} %param.43) | copy-start | bytes 3538948
  7.2 125.1 %all-gather.5.cloned.1.call-start = ((), (), s32[]{:S(2)}) async-start(), calls=%async_computation.8 | async-start | bytes 7864320 | tf_op jit(solution)/shard_map/all_gather | solution.py:106
  14.2 308.0 %reduce-scatter.12.cloned.1.call-start = ((), (), s32[]{:S(2)}) async-start(), calls=%async_computation.9 | async-start | bytes 7864320 | tf_op jit(solution)/shard_map/reduce_scatter | solution.py:121
  138.8 13.4 %copy-start.6 = (bf16[4,1024,1,192]{1,3,2,0:T(8,128)(2,1)}, bf16[4,1024,1,192]{1,3,2,0:T(8,128)(2,1)S(1)}, u32[]{:S(2)}) copy-start(bf16[4,1024,1,192]{1,3,2,0:T(8,128)(2,1)S(1)} %slice.176) | copy-start | bytes 4718596
  140.1 12.2 copy-start.13
  141.4 10.9 copy-start.17
  163.6 33.2 %copy-start.11 = (bf16[4,1024,3,64]{1,3,2,0:T(8,128)(2,1)}, bf16[4,1024,3,64]{1,3,2,0:T(8,128)(2,1)S(1)}, u32[]{:S(2)}) copy-start(bf16[4,1024,3,64]{1,3,2,0:T(8,128)(2,1)S(1)} %add_convert_fusion.5) | copy-start | bytes 4718596
  213.0 109.1 %copy-start.30 = (f32[768]{0:T(1024)S(1)}, f32[768]{0:T(1024)}, u32[]{:S(2)}) copy-start(f32[768]{0:T(1024)} %param.38) | copy-start | bytes 9220
  213.1 112.1 %copy-start.38 = (f32[768]{0:T(1024)S(1)}, f32[768]{0:T(1024)}, u32[]{:S(2)}) copy-start(f32[768]{0:T(1024)} %param.39) | copy-start | bytes 9220
  213.1 112.1 %copy-start.56 = (f32[768]{0:T(1024)S(1)}, f32[768]{0:T(1024)}, u32[]{:S(2)}) copy-start(f32[768]{0:T(1024)} %param.40) | copy-start | bytes 9220
  213.1 230.2 %all-gather.7.cloned.1.call-start = ((), (), s32[]{:S(2)}) async-start(), calls=%async_computation.10 | async-start | bytes 7864320 | tf_op jit(solution)/shard_map/all_gather | solution.py:127
  324.3 375.9 %copy-start.32 = (f32[4,256]{1,0:T(4,128)}, f32[4,256]{1,0:T(4,128)S(1)}, u32[]{:S(2)}) copy-start(f32[4,256]{1,0:T(4,128)S(1)} %broadcast_multiply_fusion) | copy-start | bytes 12292
  325.2 375.0 %copy-start.36 = (f32[4,256]{1,0:T(4,128)}, f32[4,256]{1,0:T(4,128)S(1)}, u32[]{:S(2)}) copy-start(f32[4,256]{1,0:T(4,128)S(1)} %fusion.75) | copy-start | bytes 12292
  327.3 231.0 %all-gather.9.cloned.1.call-start = ((), (), s32[]{:S(2)}) async-start(), calls=%async_computation.12 | async-start | bytes 7864320 | tf_op jit(solution)/shard_map/all_gather | solution.py:140
  327.9 230.4 %copy-start.60 = (f32[768]{0:T(1024)S(1)}, f32[768]{0:T(1024)}, u32[]{:S(2)}) copy-start(f32[768]{0:T(1024)} %param.42) | copy-start | bytes 9220
  327.9 366.4 %reduce-scatter.16.cloned.1.call-start = ((), (), s32[]{:S(2)}) async-start(), calls=%async_computation.13 | async-start | bytes 7864320 | tf_op jit(solution)/shard_map/reduce_scatter | solution.py:148
  558.3 19.7 %copy-start.58 = (bf16[768,768]{1,0:T(8,128)(2,1)S(1)}, bf16[768,768]{1,0:T(8,128)(2,1)}, u32[]{:S(2)}) copy-start(bf16[768,768]{1,0:T(8,128)(2,1)} %param.41) | copy-start | bytes 3538948
  585.2 233.7 %all-gather.11.cloned.1.call-start = ((), (), s32[]{:S(2)}) async-start(), calls=%async_computation.14 | async-start | bytes 7864320 | tf_op jit(solution)/shard_map/all_gather | solution.py:156
  702.9 341.2 %reduce-scatter.26.cloned.1.call-start = ((), (), s32[]{:S(2)}) async-start(), calls=%async_computation.19 | async-start | bytes 884736
  702.9 134.2 %copy-start.27 = (f32[4,3,512]{2,1,0:T(4,128)}, f32[4,3,512]{2,1,0:T(4,128)S(1)}, u32[]{:S(2)}) copy-start(f32[4,3,512]{2,1,0:T(4,128)S(1)} %log_add_fusion) | copy-start | bytes 73732
  703.0 166.3 %copy-start.26 = (f32[4,3,512]{2,1,0:T(4,128)}, f32[4,3,512]{2,1,0:T(4,128)S(1)}, u32[]{:S(2)}) copy-start(f32[4,3,512]{2,1,0:T(4,128)S(1)} %log_add_fusion.1) | copy-start | bytes 73732
  825.0 12.1 copy-start.12
  869.3 21.8 %copy-start.7 = (bf16[4,1024,1,192]{1,3,2,0:T(8,128)(2,1)S(1)}, bf16[4,1024,1,192]{1,3,2,0:T(8,128)(2,1)}, u32[]{:S(2)}) copy-start(bf16[4,1024,1,192]{1,3,2,0:T(8,128)(2,1)} %copy-done.6) | copy-start | bytes 4718596
  891.1 17.4 %slice-start = ((s8[6291456]{0:T(1024)(128)(4,1)}), s8[4194304]{0:T(1024)(128)(4,1)S(1)}, s32[]{:S(2)}) async-start(s8[6291456]{0:T(1024)(128)(4,1)} %bitcast.125), calls=%async_computation.20 | async-start | bytes 8388608
  899.8 8.7 copy-start.24
  899.8 8.7 slice-start.1
  911.9 168.5 %reduce-scatter.18.cloned.1.call-start = ((), (), s32[]{:S(2)}) async-start(), calls=%async_computation.15 | async-start | bytes 7864320 | tf_op jit(solution)/shard_map/reduce_scatter | solution.py:188
  912.0 12.7 copy-start.28
  912.0 12.7 copy-start.40
  924.6 38.0 %copy-start.19 = (bf16[4,3,64,1024]{3,2,1,0:T(8,128)(2,1)}, bf16[4,3,64,1024]{3,2,1,0:T(8,128)(2,1)S(1)}, u32[]{:S(2)}) copy-start(bf16[4,3,64,1024]{3,2,1,0:T(8,128)(2,1)S(1)} %add_convert_fusion.1) | copy-start | bytes 4718596
  971.4 223.7 %reduce-scatter.14.cloned.1.call-start = ((), (), s32[]{:S(2)}) async-start(), calls=%async_computation.11 | async-start | bytes 7864320 | tf_op jit(solution)/shard_map/reduce_scatter | solution.py:133
  984.3 14.6 %copy-start.61 = (u32[32]{0:T(128)S(1)}, u32[32]{0:T(128)}, u32[]{:S(2)}) copy-start(u32[32]{0:T(128)} %constant.178) | copy-start | bytes 388
  984.3 257.6 %reduce-scatter.24.cloned.1.call-start = ((), (), s32[]{:S(2)}) async-start(), calls=%async_computation.18 | async-start | bytes 2654208 | tf_op jit(solution)/shard_map/reduce_scatter | solution.py:185
  998.8 289.9 %reduce-scatter.22.cloned.1.call-start = ((), (), s32[]{:S(2)}) async-start(), calls=%async_computation.17 | async-start | bytes 2654208 | tf_op jit(solution)/shard_map/reduce_scatter | solution.py:183
  1000.8 10.5 copy-start.20
  1011.3 323.7 %reduce-scatter.20.cloned.1.call-start = ((), (), s32[]{:S(2)}) async-start(), calls=%async_computation.16 | async-start | bytes 2654208 | tf_op jit(solution)/shard_map/reduce_scatter | solution.py:180
  1025.3 55.2 %copy-start.2 = (bf16[4,256,768]{2,1,0:T(8,128)(2,1)S(1)}, bf16[4,256,768]{2,1,0:T(8,128)(2,1)}, u32[]{:S(2)}) copy-start(bf16[4,256,768]{2,1,0:T(8,128)(2,1)} %param.31) | copy-start | bytes 4718596
  1025.3 55.2 %copy-start.35 = (f32[4,256]{1,0:T(4,128)S(1)}, f32[4,256]{1,0:T(4,128)}, u32[]{:S(2)}) copy-start(f32[4,256]{1,0:T(4,128)} %copy-done.34) | copy-start | bytes 12292
  1025.3 55.2 %copy-start.44 = (f32[768]{0:T(1024)S(1)}, f32[768]{0:T(1024)}, u32[]{:S(2)}) copy-start(f32[768]{0:T(1024)} %param.33) | copy-start | bytes 9220
  1025.3 57.6 %copy-start.51 = (f32[4,256]{1,0:T(4,128)S(1)}, f32[4,256]{1,0:T(4,128)}, u32[]{:S(2)}) copy-start(f32[4,256]{1,0:T(4,128)} %copy-done.50) | copy-start | bytes 12292
  1025.3 57.6 %copy-start.31 = (f32[768]{0:T(1024)S(1)}, f32[768]{0:T(1024)}, u32[]{:S(2)}) copy-start(f32[768]{0:T(1024)} %param.38) | copy-start | bytes 9220
  1025.3 57.6 %copy-start.33 = (f32[4,256]{1,0:T(4,128)S(1)}, f32[4,256]{1,0:T(4,128)}, u32[]{:S(2)}) copy-start(f32[4,256]{1,0:T(4,128)} %copy-done.32) | copy-start | bytes 12292
  1025.3 57.6 %copy-start.37 = (f32[4,256]{1,0:T(4,128)S(1)}, f32[4,256]{1,0:T(4,128)}, u32[]{:S(2)}) copy-start(f32[4,256]{1,0:T(4,128)} %copy-done.36) | copy-start | bytes 12292
  1025.3 57.6 %copy-start.39 = (f32[768]{0:T(1024)S(1)}, f32[768]{0:T(1024)}, u32[]{:S(2)}) copy-start(f32[768]{0:T(1024)} %param.39) | copy-start | bytes 9220
  1025.3 57.6 %copy-start.42 = (f32[4,256]{1,0:T(4,128)S(1)}, f32[4,256]{1,0:T(4,128)}, u32[]{:S(2)}) copy-start(f32[4,256]{1,0:T(4,128)} %copy-done.41) | copy-start | bytes 12292
  1025.4 57.6 %copy-start.46 = (f32[4,256]{1,0:T(4,128)S(1)}, f32[4,256]{1,0:T(4,128)}, u32[]{:S(2)}) copy-start(f32[4,256]{1,0:T(4,128)} %copy-done.45) | copy-start | bytes 12292
  1025.4 57.6 %copy-start.48 = (f32[4,256]{1,0:T(4,128)S(1)}, f32[4,256]{1,0:T(4,128)}, u32[]{:S(2)}) copy-start(f32[4,256]{1,0:T(4,128)} %copy-done.47) | copy-start | bytes 12292
  1083.0 112.1 %copy-start.54 = (f32[768]{0:T(1024)S(1)}, f32[768]{0:T(1024)}, u32[]{:S(2)}) copy-start(f32[768]{0:T(1024)} %param.44) | copy-start | bytes 9220
  (29 other events, 100.6 us)
Sparse Core Ops, SparseCore 0:
  14.3 118.0 all-gather.4
  213.2 108.9 reduce-scatter.11
  327.4 115.8 all-gather.6
  444.8 113.5 all-gather.8
  585.3 108.9 reduce-scatter.15
  703.0 115.8 all-gather.10
  912.1 33.1 reduce-scatter.25
  971.5 108.8 reduce-scatter.17
  1082.8 112.2 reduce-scatter.13
  1198.9 42.9 reduce-scatter.23
  1246.2 42.4 reduce-scatter.21
  1292.5 42.4 reduce-scatter.19
where the time goes:
time: 1350 us; the launch traced here: 1340 us
  waiting for transfers between devices  892 us (66%)
  matrix products  241 us (18%)
  other arithmetic  113 us (8%)
  blocking collectives  61.8 us (5%)
  local copies, waits for them, and re-layouts  17.5 us (1%)
  between operations  16.8 us (1%)
    all_gather x1, waiting for transfers between devices, local(): resid_rows = lax.all_gather(grad_mixed_low, 'tensor', axis=1, tiled=True)  116 us
    all_gather x1, waiting for transfers between devices, local(): rows_two = lax.all_gather(normed_two, 'tensor', axis=1, tiled=True)  115 us
    all_gather x1, waiting for transfers between devices, local(): rows_one = lax.all_gather(normed_one, 'tensor', axis=1, tiled=True)  113 us
    reduce_scatter x1, waiting for transfers between devices, local(): lax.psum_scatter(norm_two_part.astype(jnp.bfloat16), 'tensor', scatter_di...  109 us
    reduce_scatter x1, waiting for transfers between devices, local(): lax.psum_scatter(attn_part.astype(jnp.bfloat16), 'tensor', scatter_dimens...  109 us
    all_gather x1, waiting for transfers between devices, local(): cot_rows = lax.all_gather(cotangent, 'tensor', axis=1, tiled=True)  104 us
    unnamed x2, blocking collectives  61.8 us
    reduce_scatter x1, waiting for transfers between devices, local(): lax.psum_scatter(down_part.astype(jnp.bfloat16), 'tensor', scatter_dimens...  56.2 us
  transfers between devices with their start and end apart: 12, of which 11 were waited for; matrix products, arithmetic and copies ran while one was open for 11% of the time, Pallas kernels for 0%

commit v1 on v0

v1 whole, which is shorter than its diff:
```python
import functools

import jax
import jax.numpy as jnp
from jax import lax
from jax.experimental import pallas as pl
from jax.experimental.pallas import tpu as pltpu
from jax.sharding import PartitionSpec as P

BF = jnp.bfloat16
F32 = jnp.float32
HEAD = 64
EPS = 1e-05
GELU_C = 0.7978845608028654
GELU_A = 0.044715
BLOCK = 256
VMEM_LIMIT = 58 * 1024 * 1024


def dot(lhs, rhs, lhs_dim, rhs_dim):
    return lax.dot_general(
        lhs, rhs, (((lhs_dim,), (rhs_dim,)), ((), ())), preferred_element_type=F32
    )


def normalize(value):
    mean = jnp.mean(value, axis=-1, keepdims=True)
    centred = value - mean
    variance = jnp.mean(centred * centred, axis=-1, keepdims=True)
    rstd = lax.rsqrt(variance + EPS)
    return centred * rstd, rstd


def norm_backward(grad, xhat, rstd, gain):
    scaled = grad * gain
    mean_e = jnp.mean(scaled, axis=-1, keepdims=True)
    mean_ex = jnp.mean(scaled * xhat, axis=-1, keepdims=True)
    return rstd * (scaled - mean_e - xhat * mean_ex)


def params(limit=VMEM_LIMIT):
    return pltpu.CompilerParams(vmem_limit_bytes=limit)


def full_spec():
    return pl.BlockSpec(memory_space=pltpu.VMEM)


def norm_one_kernel(x_ref, gain_ref, bias_ref, out_ref):
    seq = x_ref.shape[0]

    @pl.loop(0, seq // BLOCK)
    def _(step):
        rows = pl.ds(pl.multiple_of(step * BLOCK, BLOCK), BLOCK)
        xhat, _ = normalize(x_ref[rows, :].astype(F32))
        normed = xhat * gain_ref[...] + bias_ref[...]
        out_ref[:, rows] = normed.T.astype(BF)


def norm_one(x, gain, bias):
    seq, width = x.shape
    return pl.pallas_call(
        norm_one_kernel,
        out_shape=jax.ShapeDtypeStruct((width, seq), BF),
        in_specs=[full_spec()] * 3,
        out_specs=full_spec(),
        compiler_params=params(),
        name="norm_one",
        cost_estimate=pl.CostEstimate(flops=20 * seq * width, bytes_accessed=4 * seq * width, transcendentals=0),
    )(x, gain, bias)


def mask_bias(docs_col_ref, docs_row_ref, mask_ref):
    seq = mask_ref.shape[0]
    for first in range(0, seq, BLOCK):
        last = first + BLOCK
        same = docs_col_ref[0:last, :] == docs_row_ref[:, first:last]
        place_k = lax.broadcasted_iota(jnp.int32, (last, BLOCK), 0)
        place_q = first + lax.broadcasted_iota(jnp.int32, (last, BLOCK), 1)
        allowed = same & (place_k <= place_q)
        mask_ref[0:last, first:last] = jnp.where(allowed, 0.0, -1e30).astype(F32)


def attend_kernel(n1t_ref, a_ref, bq_ref, bv_ref, dcol_ref, drow_ref, qkvt_ref, at_ref, lse_ref, mask_ref):
    seq = n1t_ref.shape[1]
    part = a_ref.shape[1] // 4
    mask_bias(dcol_ref, drow_ref, mask_ref)
    for c in range(3):
        w_t = a_ref[:, c * part : (c + 1) * part].T
        proj = dot(w_t, n1t_ref[...], 1, 0)
        if c == 0:
            proj = proj + bq_ref[...]
        if c == 2:
            proj = proj + bv_ref[...]
        qkvt_ref[c * part : (c + 1) * part, :] = proj.astype(BF)
    for h in range(part // HEAD):
        q_rows = slice(h * HEAD, (h + 1) * HEAD)
        k_rows = slice(part + h * HEAD, part + (h + 1) * HEAD)
        v_rows = slice(2 * part + h * HEAD, 2 * part + (h + 1) * HEAD)
        keys = qkvt_ref[k_rows, :].T
        for first in range(0, seq, BLOCK):
            last = first + BLOCK
            q_blk = qkvt_ref[q_rows, first:last] * BF(0.125)
            scores = dot(keys[0:last], q_blk, 1, 0) + mask_ref[0:last, first:last]
            top = jnp.max(scores, axis=0, keepdims=True)
            expo = jnp.exp(scores - top)
            total = jnp.sum(expo, axis=0, keepdims=True)
            out = dot(qkvt_ref[v_rows, 0:last], expo.astype(BF), 1, 0)
            at_ref[q_rows, first:last] = (out / total).astype(BF)
            lse_ref[h : h + 1, first:last] = top + jnp.log(total)


def attend(n1t, a_k, bq, bv, dcol, drow):
    width, seq = n1t.shape
    part = a_k.shape[1] // 4
    return pl.pallas_call(
        attend_kernel,
        out_shape=(
            jax.ShapeDtypeStruct((3 * part, seq), BF),
            jax.ShapeDtypeStruct((part, seq), BF),
            jax.ShapeDtypeStruct((8, seq), F32),
        ),
        in_specs=[full_spec()] * 6,
        out_specs=(full_spec(),) * 3,
        scratch_shapes=[pltpu.VMEM((seq, seq), F32)],
        compiler_params=params(),
        name="attend",
        cost_estimate=pl.CostEstimate(
            flops=2 * seq * width * 3 * part + 4 * seq * seq * part * 4, bytes_accessed=8 * seq * width, transcendentals=seq * seq
        ),
    )(n1t, a_k, bq, bv, dcol, drow)


def attend_back_kernel(
    gmt_ref, n1t_ref, a_ref, qkvt_ref, at_ref, lse_ref, dcol_ref, drow_ref,
    gpt_ref, da_ref, gb_ref, mask_ref, gat_ref, dkv_ref,
):
    seq = n1t_ref.shape[1]
    part = a_ref.shape[1] // 4
    mask_bias(dcol_ref, drow_ref, mask_ref)
    w_out = a_ref[:, 3 * part :].T
    gat_ref[...] = dot(w_out, gmt_ref[...], 1, 0).astype(BF)
    for h in range(part // HEAD):
        q_rows = slice(h * HEAD, (h + 1) * HEAD)
        k_rows = slice(part + h * HEAD, part + (h + 1) * HEAD)
        v_rows = slice(2 * part + h * HEAD, 2 * part + (h + 1) * HEAD)
        keys = qkvt_ref[k_rows, :].T
        values = qkvt_ref[v_rows, :].T
        for first in range(0, seq, BLOCK):
            last = first + BLOCK
            q_blk = qkvt_ref[q_rows, first:last] * BF(0.125)
            g_blk = gat_ref[q_rows, first:last]
            delta = jnp.sum(
                g_blk.astype(F32) * at_ref[q_rows, first:last].astype(F32), axis=0, keepdims=True
            )
            scores = dot(keys[0:last], q_blk, 1, 0) + mask_ref[0:last, first:last]
            probs = jnp.exp(scores - lse_ref[h : h + 1, first:last])
            grad_probs = dot(values[0:last], g_blk, 1, 0)
            probs_low = probs.astype(BF)
            grad_scores = (probs * (grad_probs - delta)).astype(BF)
            gpt_ref[q_rows, first:last] = (
                0.125 * dot(qkvt_ref[k_rows, 0:last], grad_scores, 1, 0)
            ).astype(BF)
            gk = dot(q_blk, grad_scores, 1, 1)
            gv = dot(g_blk, probs_low, 1, 1)
            if first > 0:
                dkv_ref[0:HEAD, 0:first] += gk[:, 0:first]
                dkv_ref[HEAD:, 0:first] += gv[:, 0:first]
            dkv_ref[0:HEAD, first:last] = gk[:, first:last]
            dkv_ref[HEAD:, first:last] = gv[:, first:last]
        gpt_ref[k_rows, :] = dkv_ref[0:HEAD, :].astype(BF)
        gpt_ref[v_rows, :] = dkv_ref[HEAD:, :].astype(BF)
    gb_ref[:, 0:1] = jnp.sum(gpt_ref[0:part, :].astype(F32), axis=1, keepdims=True)
    gb_ref[:, 1:2] = jnp.sum(gpt_ref[2 * part : 3 * part, :].astype(F32), axis=1, keepdims=True)
    da_ref[:, 0 : 3 * part] = dot(n1t_ref[...], gpt_ref[...], 1, 1).astype(BF)
    da_ref[:, 3 * part :] = dot(gmt_ref[...], at_ref[...], 1, 1).astype(BF)


def attend_back(gmt, n1t, a_k, qkvt, at, lse, dcol, drow):
    width, seq = n1t.shape
    part = a_k.shape[1] // 4
    return pl.pallas_call(
        attend_back_kernel,
        out_shape=(
            jax.ShapeDtypeStruct((3 * part, seq), BF),
            jax.ShapeDtypeStruct((width, 4 * part), BF),
            jax.ShapeDtypeStruct((part, 2), F32),
        ),
        in_specs=[full_spec()] * 8,
        out_specs=(full_spec(),) * 3,
        scratch_shapes=[
            pltpu.VMEM((seq, seq), F32),
            pltpu.VMEM((part, seq), BF),
            pltpu.VMEM((2 * HEAD, seq), F32),
        ],
        compiler_params=params(),
        name="attend_back",
        cost_estimate=pl.CostEstimate(
            flops=2 * seq * width * 5 * part + 10 * seq * seq * part * 4, bytes_accessed=12 * seq * width, transcendentals=seq * seq
        ),
    )(gmt, n1t, a_k, qkvt, at, lse, dcol, drow)


FF_BLOCK = 256


def mlp_kernel(
    x_ref, at_ref, a_ref, m_ref, bup_ref, cot_ref, vec_ref,
    out_ref, gm_ref, gmt_ref, dm_ref, gvec_ref, gbup_ref,
    mixed_ref, n2_ref, n2t_ref, cott_ref, down_ref, gn_ref, act_ref, gpre_ref,
):
    seq, width = x_ref.shape
    n_t = at_ref.shape[0]
    part = at_ref.shape[1]
    ff = m_ref.shape[2] // 2
    step_t = pl.program_id(0)
    steps = seq // BLOCK

    @pl.when(step_t == 0)
    def _():
        down_ref[...] = jnp.zeros_like(down_ref)
        gn_ref[...] = jnp.zeros_like(gn_ref)

        @pl.loop(0, steps)
        def _(step):
            rows = pl.ds(pl.multiple_of(step * BLOCK, BLOCK), BLOCK)
            total = x_ref[rows, :].astype(F32) + vec_ref[0:1, :]
            for t in range(n_t):
                total += dot(at_ref[t, :, rows].T, a_ref[t], 1, 1)
            mixed_ref[rows, :] = total
            xhat, _ = normalize(total)
            normed = (xhat * vec_ref[1:2, :] + vec_ref[2:3, :]).astype(BF)
            n2_ref[rows, :] = normed
            n2t_ref[:, rows] = normed.T
            cott_ref[:, rows] = cot_ref[rows, :].T

    for chunk in range(ff // FF_BLOCK):
        cols = slice(chunk * FF_BLOCK, (chunk + 1) * FF_BLOCK)
        down_cols = slice(ff + chunk * FF_BLOCK, ff + (chunk + 1) * FF_BLOCK)
        w_up = m_ref[0, :, cols]
        w_down = m_ref[0, :, down_cols]
        b_up = bup_ref[0, :, cols]

        def one(step, sums):
            rows = pl.ds(pl.multiple_of(step * BLOCK, BLOCK), BLOCK)
            pre = dot(n2_ref[rows, :], w_up, 1, 0) + b_up
            grad_act = dot(cot_ref[rows, :], w_down, 1, 0)
            square = pre * pre
            curve = jnp.tanh(pre * (GELU_C + (GELU_C * GELU_A) * square))
            half = 0.5 + 0.5 * curve
            act = (pre * half).astype(BF)
            slope = half + (half - half * curve) * pre * (GELU_C + (3 * GELU_C * GELU_A) * square)
            grad_pre = (slope * grad_act).astype(BF)
            act_ref[rows, :] = act
            gpre_ref[rows, :] = grad_pre
            down_ref[rows, :] += dot(act, w_down, 1, 1)
            gn_ref[rows, :] += dot(grad_pre, w_up, 1, 1)
            return sums + jnp.sum(grad_pre.astype(F32), axis=0, keepdims=True)

        gbup_ref[0, :, cols] = lax.fori_loop(0, steps, one, jnp.zeros((1, FF_BLOCK), F32))
        dm_ref[0, :, cols] = dot(n2t_ref[...], gpre_ref[...], 1, 0).astype(BF)
        dm_ref[0, :, down_cols] = dot(cott_ref[...], act_ref[...], 1, 0).astype(BF)

    @pl.when(step_t == n_t - 1)
    def _():
        gvec_ref[...] = jnp.zeros_like(gvec_ref)

        @pl.loop(0, steps)
        def _(step):
            rows = pl.ds(pl.multiple_of(step * BLOCK, BLOCK), BLOCK)
            mixed = mixed_ref[rows, :]
            out_ref[rows, :] = (mixed + down_ref[rows, :] + vec_ref[3:4, :]).astype(BF)
            xhat, rstd = normalize(mixed)
            grad_n = gn_ref[rows, :]
            cot = cot_ref[rows, :].astype(F32)
            grad_mixed = cot + norm_backward(grad_n, xhat, rstd, vec_ref[1:2, :])
            gm_ref[rows, :] = grad_mixed
            gmt_ref[:, rows] = grad_mixed.T.astype(BF)
            gvec_ref[0:1, :] += jnp.sum(grad_mixed, axis=0, keepdims=True)
            gvec_ref[1:2, :] += jnp.sum(grad_n * xhat, axis=0, keepdims=True)
            gvec_ref[2:3, :] += jnp.sum(grad_n, axis=0, keepdims=True)
            gvec_ref[3:4, :] += jnp.sum(cot, axis=0, keepdims=True)


def mlp(x, at, w_out, m_all, b_up, cot, vecs):
    seq, width = x.shape
    n_t, part, _ = at.shape
    ff2 = m_all.shape[2]
    ff = ff2 // 2

    def fixed(shape):
        return pl.BlockSpec(shape, lambda t: (0,) * len(shape), pipeline_mode=pl.Buffered(1))

    return pl.pallas_call(
        mlp_kernel,
        grid=(n_t,),
        out_shape=(
            jax.ShapeDtypeStruct((seq, width), BF),
            jax.ShapeDtypeStruct((seq, width), F32),
            jax.ShapeDtypeStruct((width, seq), BF),
            jax.ShapeDtypeStruct((n_t, width, ff2), BF),
            jax.ShapeDtypeStruct((8, width), F32),
            jax.ShapeDtypeStruct((n_t, 1, ff), F32),
        ),
        in_specs=[
            fixed((seq, width)),
            fixed((n_t, part, seq)),
            fixed((n_t, width, part)),
            pl.BlockSpec((1, width, ff2), lambda t: (t, 0, 0)),
            pl.BlockSpec((1, 1, ff), lambda t: (t, 0, 0)),
            fixed((seq, width)),
            fixed(vecs.shape),
        ],
        out_specs=(
            fixed((seq, width)),
            fixed((seq, width)),
            fixed((width, seq)),
            pl.BlockSpec((1, width, ff2), lambda t: (t, 0, 0)),
            fixed((8, width)),
            pl.BlockSpec((1, 1, ff), lambda t: (t, 0, 0)),
        ),
        scratch_shapes=[
            pltpu.VMEM((seq, width), F32),
            pltpu.VMEM((seq, width), BF),
            pltpu.VMEM((width, seq), BF),
            pltpu.VMEM((width, seq), BF),
            pltpu.VMEM((seq, width), F32),
            pltpu.VMEM((seq, width), F32),
            pltpu.VMEM((seq, FF_BLOCK), BF),
            pltpu.VMEM((seq, FF_BLOCK), BF),
        ],
        compiler_params=params(),
        name="mlp",
        cost_estimate=pl.CostEstimate(
            flops=2 * seq * width * n_t * (6 * ff + part), bytes_accessed=20 * seq * width, transcendentals=seq * n_t * ff
        ),
    )(x, at, w_out, m_all, b_up, cot, vecs)


def input_back_kernel(gpt_ref, a_ref, x_ref, gm_ref, gain_ref, out_ref, gvec_ref):
    seq = x_ref.shape[0]
    n_t = gpt_ref.shape[0]
    part3 = gpt_ref.shape[1]
    gvec_ref[...] = jnp.zeros_like(gvec_ref)

    @pl.loop(0, seq // BLOCK)
    def _(step):
        rows = pl.ds(pl.multiple_of(step * BLOCK, BLOCK), BLOCK)
        grad_n = dot(gpt_ref[0, :, rows].T, a_ref[0, :, 0:part3], 1, 1)
        for t in range(1, n_t):
            grad_n += dot(gpt_ref[t, :, rows].T, a_ref[t, :, 0:part3], 1, 1)
        xhat, rstd = normalize(x_ref[rows, :].astype(F32))
        grad_in = gm_ref[rows, :] + norm_backward(grad_n, xhat, rstd, gain_ref[...])
        out_ref[rows, :] = grad_in.astype(BF)
        gvec_ref[0:1, :] += jnp.sum(grad_n * xhat, axis=0, keepdims=True)
        gvec_ref[1:2, :] += jnp.sum(grad_n, axis=0, keepdims=True)


def input_back(gpt, a_all, x, gm, gain):
    seq, width = x.shape
    return pl.pallas_call(
        input_back_kernel,
        out_shape=(jax.ShapeDtypeStruct((seq, width), BF), jax.ShapeDtypeStruct((8, width), F32)),
        in_specs=[full_spec()] * 5,
        out_specs=(full_spec(),) * 2,
        compiler_params=params(),
        name="input_back",
        cost_estimate=pl.CostEstimate(
            flops=2 * seq * width * gpt.shape[0] * gpt.shape[1], bytes_accessed=16 * seq * width, transcendentals=0
        ),
    )(gpt, a_all, x, gm, gain)


def gather_pieces(piece, own, n_dp, n_t):
    dp = lax.axis_index("dp")
    if n_dp != 8:
        shards = [own]
        for k in range(1, n_t):
            shards.append(lax.ppermute(own, "tensor", [((z + k) % n_t, z) for z in range(n_t)]))
        return jnp.stack(shards)
    moved = [
        lax.ppermute(piece, "tensor", [((z + k) % n_t, z) for z in range(n_t)]) for k in range(1, n_t)
    ]
    held = {0: jnp.stack(moved)}
    for mask in (2, 4, 6):
        held[mask] = lax.ppermute(held[0], "dp", [(i, i ^ mask) for i in range(n_dp)])
    for mask in (0, 2, 4, 6):
        held[mask + 1] = lax.ppermute(held[mask], "dp", [(i, i ^ 1) for i in range(n_dp)])
    rows = piece.shape[0]
    whole = jnp.zeros((n_t - 1,) + own.shape, own.dtype)
    for mask, part in held.items():
        whole = lax.dynamic_update_slice(whole, part, (0, (dp ^ mask) * rows, 0))
    return jnp.concatenate([own[None], whole])


def scatter_sum(grads, n_dp, n_t):
    dp = lax.axis_index("dp")
    rows = grads.shape[1] // n_dp
    cols = grads.shape[2]
    if n_dp != 8:
        summed = lax.psum_scatter(grads, "dp", scatter_dimension=1, tiled=True)
    else:
        split = grads.reshape(n_t, n_dp // 2, 2, rows, cols)
        core = dp % 2
        keep = lax.dynamic_index_in_dim(split, core, 2, keepdims=False)
        send = lax.dynamic_index_in_dim(split, 1 - core, 2, keepdims=False)
        got = lax.ppermute(send, "dp", [(i, i ^ 1) for i in range(n_dp)])
        half = (keep.astype(F32) + got.astype(F32)).astype(BF)
        total = lax.dynamic_index_in_dim(half, dp // 2, 1, keepdims=False).astype(F32)
        for mask in (2, 4, 6):
            part = lax.dynamic_index_in_dim(half, (dp ^ mask) // 2, 1, keepdims=False)
            total += lax.ppermute(part, "dp", [(i, i ^ mask) for i in range(n_dp)]).astype(F32)
        summed = total.astype(BF)
    result = summed[0].astype(F32)
    for k in range(1, n_t):
        result += lax.ppermute(
            summed[k], "tensor", [(z, (z + k) % n_t) for z in range(n_t)]
        ).astype(F32)
    return result


def to_rows(blocks, n_t):
    return lax.all_to_all(blocks, "tensor", 0, 1, tiled=True)


def to_positions(rows, n_t):
    return lax.all_to_all(rows, "tensor", 1, 0, tiled=True)


def local(n_dp, n_t, inputs, doc_ids, ln1_gain, ln1_bias, w_qkv, b_qv, w_out, out_bias, ln2_gain, ln2_bias,
          w_up, b_up, w_down, down_bias, cotangent):
    width = inputs.shape[2]
    part = w_out.shape[0]
    dp = lax.axis_index("dp")
    tensor = lax.axis_index("tensor")
    own_rows = inputs.shape[0] // n_t

    own_a = jnp.concatenate([w_qkv.reshape(width, 3 * part), w_out.T], axis=1)
    own_m = jnp.concatenate([w_up, w_down.T], axis=1)
    rows = width // n_dp
    piece_a = lax.dynamic_slice_in_dim(own_a, dp * rows, rows, 0)
    piece_m = lax.dynamic_slice_in_dim(own_m, dp * rows, rows, 0)
    a_all = gather_pieces(piece_a, own_a, n_dp, n_t)
    x_rows = to_rows(inputs, n_t)
    cot_rows = to_rows(cotangent, n_t)
    m_all = gather_pieces(piece_m, own_m, n_dp, n_t)

    small = jnp.concatenate([b_qv.reshape(-1), b_up])
    smalls = [small]
    for k in range(1, n_t):
        smalls.append(lax.ppermute(small, "tensor", [((z + k) % n_t, z) for z in range(n_t)]))
    smalls = jnp.stack(smalls)
    bq = smalls[:, 0:part, None]
    bv = smalls[:, part : 2 * part, None]
    bup = smalls[:, None, 2 * part :]
    vecs = jnp.stack([out_bias, ln2_gain, ln2_bias, down_bias])
    doc_rows = lax.dynamic_slice_in_dim(doc_ids, tensor * own_rows, own_rows, 0)

    outs, grads_in, das, dms, gvecs, gins, gbs, gbups = [], [], [], [], [], [], [], []
    for r in range(own_rows):
        x = x_rows[r]
        drow = doc_rows[r][None, :]
        dcol = doc_rows[r][:, None]
        n1t = norm_one(x, ln1_gain[None], ln1_bias[None])
        fwd = [attend(n1t, a_all[k], bq[k], bv[k], dcol, drow) for k in range(n_t)]
        at = jnp.stack([f[1] for f in fwd])
        out, gm, gmt, dm, gvec, gbup = mlp(x, at, a_all[:, :, 3 * part :], m_all, bup, cot_rows[r], vecs)
        back = [
            attend_back(gmt, n1t, a_all[k], fwd[k][0], fwd[k][1], fwd[k][2], dcol, drow) for k in range(n_t)
        ]
        gpt = jnp.stack([b[0] for b in back])
        grad_in, gin = input_back(gpt, a_all, x, gm, ln1_gain[None])
        outs.append(out)
        grads_in.append(grad_in)
        das.append(jnp.stack([b[1] for b in back]))
        gbs.append(jnp.stack([b[2] for b in back]))
        dms.append(dm)
        gvecs.append(gvec)
        gins.append(gin)
        gbups.append(gbup)

    def total(items):
        if len(items) == 1:
            return items[0]
        return sum(item.astype(F32) for item in items).astype(items[0].dtype)

    block_out = to_positions(jnp.stack(outs), n_t)
    grad_inputs = to_positions(jnp.stack(grads_in), n_t)
    share_m = scatter_sum(total(dms), n_dp, n_t)
    share_a = scatter_sum(total(das), n_dp, n_t)
    gvec, gin, gb, gbup = total(gvecs), total(gins), total(gbs), total(gbups)

    ff = w_up.shape[1]
    spread = jnp.concatenate([gin[0:2], gvec[0:4]])
    spread = spread.reshape(6, n_dp * n_t, width // (n_dp * n_t)).transpose(1, 0, 2).reshape(n_dp, n_t, -1)
    shard = jnp.concatenate(
        [
            gb.transpose(0, 2, 1).reshape(n_t, 2, n_dp, part // n_dp).transpose(2, 0, 1, 3).reshape(n_dp, n_t, -1),
            gbup.reshape(n_t, n_dp, ff // n_dp).transpose(1, 0, 2),
        ],
        axis=2,
    )
    shard = jnp.roll(shard, tensor, axis=1)
    both = jnp.concatenate([spread, shard], axis=2).reshape(n_dp * n_t, -1)
    mine = lax.psum_scatter(both, ("dp", "tensor"), scatter_dimension=0, tiled=True)[0]
    each = width // (n_dp * n_t)
    vec = mine[0 : 6 * each].reshape(6, each)
    share_b_qv = mine[6 * each : 6 * each + 2 * (part // n_dp)].reshape(2, part // n_dp)
    share_b_up = mine[6 * each + 2 * (part // n_dp) :]
    share_w_qkv = share_a[:, 0 : 3 * part].reshape(rows, 3, part)
    share_w_out = share_a[:, 3 * part :].T
    share_w_up = share_m[:, 0:ff]
    share_w_down = share_m[:, ff:].T
    return (
        block_out,
        grad_inputs,
        vec[0],
        vec[1],
        share_w_qkv,
        share_b_qv,
        share_w_out,
        vec[2],
        vec[3],
        vec[4],
        share_w_up,
        share_b_up,
        share_w_down,
        vec[5],
    )


def solution(mesh):
    return jax.shard_map(
        functools.partial(local, mesh.shape["dp"], mesh.shape["tensor"]),
        mesh=mesh,
        in_specs=(
            P("dp", "tensor", None),
            P("dp", None),
            P(),
            P(),
            P(None, None, "tensor"),
            P(None, "tensor"),
            P("tensor", None),
            P(),
            P(),
            P(),
            P(None, "tensor"),
            P("tensor"),
            P("tensor", None),
            P(),
            P("dp", "tensor", None),
        ),
        out_specs=(
            P("dp", "tensor", None),
            P("dp", "tensor", None),
            P(("dp", "tensor")),
            P(("dp", "tensor")),
            P("dp", None, "tensor"),
            P(None, ("tensor", "dp")),
            P("tensor", "dp"),
            P(("dp", "tensor")),
            P(("dp", "tensor")),
            P(("dp", "tensor")),
            P("dp", "tensor"),
            P(("tensor", "dp")),
            P("tensor", "dp"),
            P(("dp", "tensor")),
        ),
        check_vma=False,
    )
```

time: 1350 us -> 600 us (0.44)
  waiting for transfers between devices: 892 us -> 99.7 us
  matrix products: 241 us -> 0 us
  Pallas kernels: 0 us -> 167 us
  local copies, waits for them, and re-layouts: 17.5 us -> 86.6 us
  starting transfers between devices: 0.49 us -> 65.8 us
  other arithmetic: 113 us -> 64.8 us
  blocking collectives: 61.8 us -> 103 us
  between operations: 16.8 us -> 1.6 us
    all_gather x4 -> x0, waiting for transfers between devices: 449 us -> none  [the longest x1 116 us: local(): resid_rows = lax.all_gather(grad_mixed_low, 'tensor', axis=1, tiled=True)]
    reduce_scatter x7 -> x0, waiting for transfers between devices: 442 us -> none  [the longest x1 109 us: local(): lax.psum_scatter(norm_two_part.astype(jnp.bfloat16), 'tensor', scatter_di...]
    dot_general x24 -> x0, matrix products: 241 us -> none  [the longest x2 32.2 us: attend_backward(): jnp.einsum('rqhe,rkhe->rhqk', grad_blk, value_h, preferred_element_type=j...]
    pallas_call x0 -> x11, Pallas kernels: none -> 167 us  [the longest x1 64 us: mlp(): pl.pallas_call(mlp_kernel, grid=(n_t,), out_shape=(jax.ShapeDtypeStruct((...]
    ppermute x0 -> x37, waiting for transfers between devices: none -> 85.9 us  [the longest x6 32.5 us: gather_pieces(): lax.ppermute(held[0], 'dp', [(i, i ^ mask) for i in range(n_dp)])]
    convert_element_type x8 -> x4, other arithmetic: 58.2 us -> 11.9 us  [the longest x2 7.04 us: scatter_sum(): half = (keep.astype(F32) + got.astype(F32)).astype(BF)]
    reduce_sum x11 -> x0, other arithmetic: 45.7 us -> none  [the longest x2 22.7 us: attend_forward(): total = jnp.sum(expo, axis=-1, keepdims=True)]
    ppermute x0 -> x37, starting transfers between devices: none -> 45 us  [the longest x6 15.3 us: gather_pieces(): lax.ppermute(piece, 'tensor', [((z + k) % n_t, z) for z in range(n_t)])]
  transfers between devices with their start and end apart: 12 -> 41, of which waited for: 11 -> 8; matrix products, arithmetic and copies ran while one was open for 11% -> 23% of each run, Pallas kernels for 0% -> 18%
where the time goes in v1:
time: 600 us; the launch traced here: 589 us
  Pallas kernels  167 us (28%)
  blocking collectives  103 us (17%)
  waiting for transfers between devices  99.7 us (17%)
  local copies, waits for them, and re-layouts  86.6 us (14%)
  starting transfers between devices  65.8 us (11%)
  other arithmetic  64.8 us (11%)
    unnamed x1, blocking collectives  103 us
    pallas_call x1, Pallas kernels, mlp(): pl.pallas_call(mlp_kernel, grid=(n_t,), out_shape=(jax.ShapeDtypeStruct((...  64 us
    pallas_call x4, Pallas kernels, attend_back(): pl.pallas_call(attend_back_kernel, out_shape=(jax.ShapeDtypeStruct((3 * p...  48.9 us
    pallas_call x4, Pallas kernels, attend(): pl.pallas_call(attend_kernel, out_shape=(jax.ShapeDtypeStruct((3 * part,...  36.6 us
    ppermute x6, waiting for transfers between devices, gather_pieces(): lax.ppermute(held[0], 'dp', [(i, i ^ mask) for i in range(n_dp)])  32.5 us
    ppermute x6, waiting for transfers between devices, gather_pieces(): lax.ppermute(piece, 'tensor', [((z + k) % n_t, z) for z in range(n_t)])  28.1 us
    unnamed x90, local copies, waits for them, and re-layouts  24.3 us
    unnamed x4, other arithmetic  23.2 us
  transfers between devices with their start and end apart: 41, of which 8 were waited for; matrix products, arithmetic and copies ran while one was open for 23% of the time, Pallas kernels for 18%

profile of v1, /device:TPU:0, one launch (start us, length us, event | category | flops | bytes accessed | tf_op | source)
XLA Modules:
  0.0 588.8 jit_solution(5364751089387130426)
XLA Ops:
  3.1 5.0 collective-permute-start.13
  11.3 2.5 collective-permute-start.11
  15.8 4.4 all-to-all-start
  31.0 5.8 collective-permute-start.1
  40.0 2.7 collective-permute-start
  44.1 28.1 %collective-permute-done.1 = bf16[96,768]{1,0:T(8,128)(2,1)S(1)} collective-permute-done((bf16[96,768]{1,0:T(8,128)(2,1)S(1)}, bf16[96,768]{1,0:T(8,128)(2,1)S(1)}, u32[]{:S(2)}, u32[]{:S(2)}) %collective-permute-start.1) | collective-permute-done | bytes 147488 | tf_op jit(solution)/shard_map/ppermute | solution.py:382
  86.1 3.4 broadcast_in_dim.29
  89.5 2.3 pad_maximum_fusion.7
  103.2 2.5 pad_maximum_fusion.1.a_ref
  107.3 6.9 %collective-permute-done.16 = bf16[3,96,1536]{2,1,0:T(8,128)(2,1)S(1)} collective-permute-done((bf16[3,96,1536]{2,1,0:T(8,128)(2,1)S(1)}, bf16[3,96,1536]{2,1,0:T(8,128)(2,1)S(1)}, u32[]{:S(2)}, u32[]{:S(2)}) %collective-permute-start.16) | collective-permute-done | bytes 884768 | tf_op jit(solution)/shard_map/ppermute | solution.py:386
  115.2 24.1 %collective-permute-done.17 = bf16[3,96,1536]{2,1,0:T(8,128)(2,1)S(1)} collective-permute-done((bf16[3,96,1536]{2,1,0:T(8,128)(2,1)S(1)}, bf16[3,96,1536]{2,1,0:T(8,128)(2,1)S(1)}, u32[]{:S(2)}, u32[]{:S(2)}) %collective-permute-start.17) | collective-permute-done | bytes 884768 | tf_op jit(solution)/shard_map/ppermute | solution.py:386
  140.8 2.2 constant_dynamic-update-slice_fusion.4
  146.0 6.8 %all-to-all-start.1 = ((bf16[4,256,768]{2,1,0:T(8,128)(2,1)}), bf16[4,256,768]{2,1,0:T(8,128)(2,1)}, u32[]{:S(2)}, u32[]{:S(2)}) async-start(bf16[4,256,768]{2,1,0:T(8,128)(2,1)} %param.29), calls=%async_computation.1 | async-start | bytes 3145728 | tf_op jit(solution)/shard_map/all_to_all | solution.py:423
  153.7 7.5 %pad_maximum_fusion.m_ref = bf16[4,768,1536]{2,1,0:T(8,128)(2,1)} fusion(bf16[3,768,1536]{2,1,0:T(8,128)(2,1)} %constant_dynamic-update-slice_fusion, bf16[1,768,1536]{2,1,0:T(8,128)(2,1)S(1)} %copy-done.5), kind=kLoop, calls=%fused_computation | loop fusion | flops 4718592 | bytes 18874368 | tf_op jit(solution)/shard_map/concatenate | solution.py:393
  161.2 4.6 norm_one.1.n1t_ref
  165.8 9.1 %attend.5 = (bf16[576,1024]{1,0:T(8,128)(2,1)}, bf16[192,1024]{1,0:T(8,128)(2,1)}, f32[8,1024]{1,0:T(8,128)}) custom-call(bf16[768,1024]{1,0:T(8,128)(2,1)} %norm_one.1.n1t_ref, bf16[768,768]{1,0:T(8,128)(2,1)} %get-tuple-element.159.a_ref, f32[192,1]{1,0:T(8,128)} %copy.187.bq_ref, f32[192,1]{1,0:T(8,128)} %copy.188.bv_ref, s32[1024,1]{1,0:T(8,128)} %copy.186.dcol_ref, ...), custom_call_target="tpu_custom_call" | custom-call | flops 4127195136 | bytes 6291456 | tf_op jit(solution)/shard_map/attend/pallas_call | solution.py:116
  174.9 9.1 %attend.6 = (bf16[576,1024]{1,0:T(8,128)(2,1)}, bf16[192,1024]{1,0:T(8,128)(2,1)}, f32[8,1024]{1,0:T(8,128)}) custom-call(bf16[768,1024]{1,0:T(8,128)(2,1)} %norm_one.1.n1t_ref, bf16[768,768]{1,0:T(8,128)(2,1)} %get-tuple-element.161.a_ref, f32[192,1]{1,0:T(8,128)} %copy.190.bq_ref, f32[192,1]{1,0:T(8,128)} %copy.191.bv_ref, s32[1024,1]{1,0:T(8,128)} %copy.186.dcol_ref, ...), custom_call_target="tpu_custom_call" | custom-call | flops 4127195136 | bytes 6291456 | tf_op jit(solution)/shard_map/attend/pallas_call | solution.py:116
  184.0 9.3 %attend.7 = (bf16[576,1024]{1,0:T(8,128)(2,1)}, bf16[192,1024]{1,0:T(8,128)(2,1)}, f32[8,1024]{1,0:T(8,128)}) custom-call(bf16[768,1024]{1,0:T(8,128)(2,1)} %norm_one.1.n1t_ref, bf16[768,768]{1,0:T(8,128)(2,1)} %get-tuple-element.160.a_ref, f32[192,1]{1,0:T(8,128)} %copy.193.bq_ref, f32[192,1]{1,0:T(8,128)} %copy.194.bv_ref, s32[1024,1]{1,0:T(8,128)} %copy.186.dcol_ref, ...), custom_call_target="tpu_custom_call" | custom-call | flops 4127195136 | bytes 6291456 | tf_op jit(solution)/shard_map/attend/pallas_call | solution.py:116
  193.2 9.2 %attend.4 = (bf16[576,1024]{1,0:T(8,128)(2,1)}, bf16[192,1024]{1,0:T(8,128)(2,1)}, f32[8,1024]{1,0:T(8,128)}) custom-call(bf16[768,1024]{1,0:T(8,128)(2,1)} %norm_one.1.n1t_ref, bf16[768,768]{1,0:T(8,128)(2,1)} %pad_maximum_fusion.6.a_ref, f32[192,1]{1,0:T(8,128)} %copy.184.bq_ref, f32[192,1]{1,0:T(8,128)} %copy.185.bv_ref, s32[1024,1]{1,0:T(8,128)} %copy.186.dcol_ref, ...), custom_call_target="tpu_custom_call" | custom-call | flops 4127195136 | bytes 6291456 | tf_op jit(solution)/shard_map/attend/pallas_call | solution.py:116
  202.4 2.3 pad_maximum_fusion.5.at_ref
  204.8 64.0 %mlp.1 = (bf16[1024,768]{1,0:T(8,128)(2,1)}, f32[1024,768]{1,0:T(8,128)}, bf16[768,1024]{1,0:T(8,128)(2,1)}, bf16[4,768,1536]{2,1,0:T(8,128)(2,1)}, f32[8,768]{1,0:T(8,128)}, /*index=5*/f32[4,1,768]{2,1,0:T(1,128)}) custom-call(bf16[1024,768]{1,0:T(8,128)(2,1)} %bitcast.2.x_ref, bf16[4,192,1024]{2,1,0:T(8,128)(2,1)} %pad_maximum_fusion.5.at_ref, ...), custom_call_target="tpu_custom_call" | custom-call | flops 30198988800 | bytes 15728640 | tf_op jit(solution)/shard_map/mlp/pallas_call | solution.py:294
  268.8 6.7 %constant_dynamic-slice_fusion.1 = (bf16[4,4,1,96,1536]{4,3,2,1,0:T(8,128)(2,1)}, bf16[4,4,1,96,1536]{4,3,2,1,0:T(8,128)(2,1)S(1)}) fusion(bf16[4,4,2,96,1536]{4,3,2,1,0:T(8,128)(2,1)} %bitcast.154, s32[]{:T(128)S(6)} %select_n.115, s32[]{:T(128)S(6)} %select_n.116), kind=kLoop, calls=%fused_computation.83 | loop fusion | bytes 18874376 | tf_op jit(solution)/shard_map/jit(dynamic_index_in_dim)/dynamic_slice | solution.py:405
  275.5 2.5 copy.237
  278.1 12.0 %attend_back.4 = (bf16[576,1024]{1,0:T(8,128)(2,1)}, bf16[768,768]{1,0:T(8,128)(2,1)}, f32[192,2]{1,0:T(8,128)}) custom-call(bf16[768,1024]{1,0:T(8,128)(2,1)} %get-tuple-element.51.gmt_ref, bf16[768,1024]{1,0:T(8,128)(2,1)} %norm_one.1.n1t_ref, bf16[768,768]{1,0:T(8,128)(2,1)} %pad_maximum_fusion.6.a_ref, bf16[576,1024]{1,0:T(8,128)(2,1)} %get-tuple-element.52.qkvt_ref, ...), custom_call_target="tpu_custom_call" | custom-call | flops 9563013120 | bytes 9437184 | tf_op jit(solution)/shard_map/attend_back/pallas_call | solution.py:182
  290.1 12.2 %attend_back.5 = (bf16[576,1024]{1,0:T(8,128)(2,1)}, bf16[768,768]{1,0:T(8,128)(2,1)}, f32[192,2]{1,0:T(8,128)}) custom-call(bf16[768,1024]{1,0:T(8,128)(2,1)} %get-tuple-element.51.gmt_ref, bf16[768,1024]{1,0:T(8,128)(2,1)} %norm_one.1.n1t_ref, bf16[768,768]{1,0:T(8,128)(2,1)} %get-tuple-element.159.a_ref, bf16[576,1024]{1,0:T(8,128)(2,1)} %get-tuple-element.55.qkvt_ref, ...), custom_call_target="tpu_custom_call" | custom-call | flops 9563013120 | bytes 9437184 | tf_op jit(solution)/shard_map/attend_back/pallas_call | solution.py:182
  302.3 12.0 %attend_back.6 = (bf16[576,1024]{1,0:T(8,128)(2,1)}, bf16[768,768]{1,0:T(8,128)(2,1)}, f32[192,2]{1,0:T(8,128)}) custom-call(bf16[768,1024]{1,0:T(8,128)(2,1)} %get-tuple-element.51.gmt_ref, bf16[768,1024]{1,0:T(8,128)(2,1)} %norm_one.1.n1t_ref, bf16[768,768]{1,0:T(8,128)(2,1)} %get-tuple-element.161.a_ref, bf16[576,1024]{1,0:T(8,128)(2,1)} %get-tuple-element.58.qkvt_ref, ...), custom_call_target="tpu_custom_call" | custom-call | flops 9563013120 | bytes 9437184 | tf_op jit(solution)/shard_map/attend_back/pallas_call | solution.py:182
  314.4 12.6 %attend_back.7 = (bf16[576,1024]{1,0:T(8,128)(2,1)}, bf16[768,768]{1,0:T(8,128)(2,1)}, f32[192,2]{1,0:T(8,128)}) custom-call(bf16[768,1024]{1,0:T(8,128)(2,1)} %get-tuple-element.51.gmt_ref, bf16[768,1024]{1,0:T(8,128)(2,1)} %norm_one.1.n1t_ref, bf16[768,768]{1,0:T(8,128)(2,1)} %get-tuple-element.160.a_ref, bf16[576,1024]{1,0:T(8,128)(2,1)} %get-tuple-element.61.qkvt_ref, ...), custom_call_target="tpu_custom_call" | custom-call | flops 9563013120 | bytes 9437184 | tf_op jit(solution)/shard_map/attend_back/pallas_call | solution.py:182
  327.0 3.5 pad_maximum_fusion.2.gpt_ref
  330.5 12.9 %input_back.1 = (bf16[1024,768]{1,0:T(8,128)(2,1)}, f32[8,768]{1,0:T(8,128)}) custom-call(bf16[4,576,1024]{2,1,0:T(8,128)(2,1)} %pad_maximum_fusion.2.gpt_ref, bf16[4,768,768]{2,1,0:T(8,128)(2,1)} %pad_maximum_fusion.1.a_ref, bf16[1024,768]{1,0:T(8,128)(2,1)} %bitcast.2.x_ref, f32[1024,768]{1,0:T(8,128)} %get-tuple-element.64.gm_ref, ...), custom_call_target="tpu_custom_call" | custom-call | flops 3623878656 | bytes 12582912 | tf_op jit(solution)/shard_map/input_back/pallas_call | solution.py:361
  343.4 3.8 copy.240
  347.7 11.6 %reduce.18 = bf16[1024,768]{1,0:T(8,128)(2,1)} reduce(bf16[1024,1,768]{2,1,0:T(2,128)(2,1)S(1)} %bitcast.148, bf16[]{:T(256)} %broadcast.15), dimensions={1}, to_apply=%bitcast.144.reduce_sub_computation | reduce | bytes 3145730
  359.3 3.8 reshape.157
  363.1 5.2 all-to-all-start.3
  373.1 3.8 copy.241
  376.9 11.6 %reduce.17 = bf16[1024,768]{1,0:T(8,128)(2,1)} reduce(bf16[1024,1,768]{2,1,0:T(2,128)(2,1)S(1)} %bitcast.149, bf16[]{:T(256)} %broadcast.15), dimensions={1}, to_apply=%bitcast.145.reduce_sub_computation | reduce | bytes 3145730
  388.6 3.7 reshape.155
  392.3 13.8 %all-to-all-done.3 = bf16[4,2,98304]{2,1,0:T(2,128)(2,1)} async-done(((bf16[4,2,98304]{2,1,0:T(2,128)(2,1)}), bf16[4,2,98304]{2,1,0:T(2,128)(2,1)}, u32[]{:S(2)}, u32[]{:S(2)}) %all-to-all-start.3) | async-done | bytes 1572896 | tf_op jit(solution)/shard_map/all_to_all | solution.py:427
  406.1 4.5 all-to-all-start.2
  410.6 3.2 fusion.1
  416.3 3.8 fusion
  427.8 3.7 collective-permute-done.24
  435.0 103.1 %all-reduce = f32[32,288]{0,1:T(8,128)S(1)} all-reduce(f32[32,288]{0,1:T(8,128)S(1)} %pad_maximum_fusion.9), channel_id=2, replica_groups=mesh['dp'=8,'tensor'=4] {'dp','tensor'}, use_global_device_ids=true, to_apply=%region_0.1.clone | all-reduce | flops 9216 | bytes 73728
  540.4 3.0 reshape.158
  544.9 3.1 reshape.156
  555.2 2.9 fusion.5
  560.3 2.8 collective-permute-start.36
  563.2 12.2 %collective-permute-done.28 = bf16[96,768]{1,0:T(8,128)(2,1)S(1)} collective-permute-done((bf16[96,768]{1,0:T(8,128)(2,1)S(1)}, bf16[96,768]{1,0:T(8,128)(2,1)S(1)}, u32[]{:S(2)}, u32[]{:S(2)}) %collective-permute-start.28) | collective-permute-done | bytes 147488 | tf_op jit(solution)/shard_map/ppermute | solution.py:416
  577.4 9.2 %collective-permute-done.35 = bf16[96,1536]{1,0:T(8,128)(2,1)S(1)} collective-permute-done((bf16[96,1536]{1,0:T(8,128)(2,1)S(1)}, bf16[96,1536]{1,0:T(8,128)(2,1)S(1)}, u32[]{:S(2)}, u32[]{:S(2)}) %collective-permute-start.35) | collective-permute-done | bytes 294944 | tf_op jit(solution)/shard_map/ppermute | solution.py:416
  (245 shorter events, 91.9 us)
Async XLA Ops:
  0.6 25.4 %copy-start = (s32[4,1024]{1,0:T(4,128)S(1)}, s32[4,1024]{1,0:T(4,128)}, u32[]{:S(2)}) copy-start(s32[4,1024]{1,0:T(4,128)} %param.16) | copy-start | bytes 49156
  3.1 73.8 %collective-permute-start.13 = (bf16[96,1536]{1,0:T(8,128)(2,1)}, bf16[96,1536]{1,0:T(8,128)(2,1)}, u32[]{:S(2)}, u32[]{:S(2)}) collective-permute-start(bf16[96,1536]{1,0:T(8,128)(2,1)} %fusion.12), channel_id=1, source_target_pairs={{1,0},{2,1},{3,2},{0,3},{5,4},{6,5},{7,6},{4,7},{9,8},{10,9},{11,1... | collective-permute-start | bytes 884744 | tf_op jit(solution)/shard_map/ppermute | solution.py:382
  8.2 77.9 %collective-permute-start.14 = (bf16[96,1536]{1,0:T(8,128)(2,1)}, bf16[96,1536]{1,0:T(8,128)(2,1)}, u32[]{:S(2)}, u32[]{:S(2)}) collective-permute-start(bf16[96,1536]{1,0:T(8,128)(2,1)} %fusion.12), channel_id=1, source_target_pairs={{2,0},{3,1},{0,2},{1,3},{6,4},{7,5},{4,6},{5,7},{10,8},{11,9},{8,1... | collective-permute-start | bytes 884744 | tf_op jit(solution)/shard_map/ppermute | solution.py:382
  10.9 20.2 %collective-permute-start.10 = (f32[1152]{0:T(1024)}, f32[1152]{0:T(1024)}, u32[]{:S(2)}, u32[]{:S(2)}) collective-permute-start(f32[1152]{0:T(1024)} %constant_dynamic-update-slice_fusion.16), channel_id=1, source_target_pairs={{1,0},{2,1},{3,2},{0,3},{5,4},{6,5},{7,6},{4,7},{9,8},{10,9},{11,1... | collective-permute-start | bytes 13832 | tf_op jit(solution)/shard_map/ppermute | solution.py:451
  11.3 26.9 %collective-permute-start.11 = (f32[1152]{0:T(1024)}, f32[1152]{0:T(1024)}, u32[]{:S(2)}, u32[]{:S(2)}) collective-permute-start(f32[1152]{0:T(1024)} %constant_dynamic-update-slice_fusion.16), channel_id=1, source_target_pairs={{2,0},{3,1},{0,2},{1,3},{6,4},{7,5},{4,6},{5,7},{10,8},{11,9},{8,1... | collective-permute-start | bytes 13832 | tf_op jit(solution)/shard_map/ppermute | solution.py:451
  13.8 26.2 %collective-permute-start.12 = (f32[1152]{0:T(1024)}, f32[1152]{0:T(1024)}, u32[]{:S(2)}, u32[]{:S(2)}) collective-permute-start(f32[1152]{0:T(1024)} %constant_dynamic-update-slice_fusion.16), channel_id=1, source_target_pairs={{3,0},{0,1},{1,2},{2,3},{7,4},{4,5},{5,6},{6,7},{11,8},{8,9},{9,10... | collective-permute-start | bytes 13832 | tf_op jit(solution)/shard_map/ppermute | solution.py:451
  15.8 130.2 %all-to-all-start = ((bf16[4,256,768]{2,1,0:T(8,128)(2,1)}), bf16[4,256,768]{2,1,0:T(8,128)(2,1)}, u32[]{:S(2)}, u32[]{:S(2)}) async-start(bf16[4,256,768]{2,1,0:T(8,128)(2,1)} %param.15), calls=%async_computation | async-start | bytes 3145728 | tf_op jit(solution)/shard_map/all_to_all | solution.py:423
  24.7 48.1 %copy-start.23 = (f32[1,1152]{1,0:T(1,128)}, f32[1,1152]{1,0:T(1,128)S(1)}, u32[]{:S(2)}) copy-start(f32[1,1152]{1,0:T(1,128)S(1)} %stack.120) | copy-start | bytes 13828
  31.0 41.2 %collective-permute-start.1 = (bf16[96,768]{1,0:T(8,128)(2,1)S(1)}, bf16[96,768]{1,0:T(8,128)(2,1)S(1)}, u32[]{:S(2)}, u32[]{:S(2)}) collective-permute-start(bf16[96,768]{1,0:T(8,128)(2,1)S(1)} %fusion.15), channel_id=1, source_target_pairs={{2,0},{3,1},{0,2},{1,3},{6,4},{7,5},{4,6},{5,7},{10,8},{11,9},{8,1... | collective-permute-start | bytes 442376 | tf_op jit(solution)/shard_map/ppermute | solution.py:382
  37.5 36.3 %copy-start.24 = (f32[1,1152]{1,0:T(1,128)}, f32[1,1152]{1,0:T(1,128)S(1)}, u32[]{:S(2)}) copy-start(f32[1,1152]{1,0:T(1,128)S(1)} %stack.126) | copy-start | bytes 13828
  38.2 34.6 %collective-permute-start.2 = (bf16[96,768]{1,0:T(8,128)(2,1)S(1)}, bf16[96,768]{1,0:T(8,128)(2,1)S(1)}, u32[]{:S(2)}, u32[]{:S(2)}) collective-permute-start(bf16[96,768]{1,0:T(8,128)(2,1)S(1)} %fusion.15), channel_id=1, source_target_pairs={{3,0},{0,1},{1,2},{2,3},{7,4},{4,5},{5,6},{6,7},{11,8},{8,9},{9,10... | collective-permute-start | bytes 442376 | tf_op jit(solution)/shard_map/ppermute | solution.py:382
  40.0 33.9 %copy-start.25 = (f32[1,1152]{1,0:T(1,128)}, f32[1,1152]{1,0:T(1,128)S(1)}, u32[]{:S(2)}) copy-start(f32[1,1152]{1,0:T(1,128)S(1)} %stack.128) | copy-start | bytes 13828
  40.0 32.8 %collective-permute-start = (bf16[96,768]{1,0:T(8,128)(2,1)S(1)}, bf16[96,768]{1,0:T(8,128)(2,1)S(1)}, u32[]{:S(2)}, u32[]{:S(2)}) collective-permute-start(bf16[96,768]{1,0:T(8,128)(2,1)S(1)} %fusion.15), channel_id=1, source_target_pairs={{1,0},{2,1},{3,2},{0,3},{5,4},{6,5},{7,6},{4,7},{9,8},{10,9},{11,1... | collective-permute-start | bytes 442376 | tf_op jit(solution)/shard_map/ppermute | solution.py:382
  43.5 33.9 %copy-start.26 = (f32[1,1152]{1,0:T(1,128)}, f32[1,1152]{1,0:T(1,128)S(1)}, u32[]{:S(2)}) copy-start(f32[1,1152]{1,0:T(1,128)S(1)} %stack.130) | copy-start | bytes 13828
  72.2 13.8 %collective-permute-start.15 = (bf16[96,1536]{1,0:T(8,128)(2,1)}, bf16[96,1536]{1,0:T(8,128)(2,1)}, u32[]{:S(2)}, u32[]{:S(2)}) collective-permute-start(bf16[96,1536]{1,0:T(8,128)(2,1)} %fusion.12), channel_id=1, source_target_pairs={{3,0},{0,1},{1,2},{2,3},{7,4},{4,5},{5,6},{6,7},{11,8},{8,9},{9,10... | collective-permute-start | bytes 884744 | tf_op jit(solution)/shard_map/ppermute | solution.py:382
  73.9 19.3 %collective-permute-start.3 = (bf16[3,96,768]{2,1,0:T(8,128)(2,1)}, bf16[3,96,768]{2,1,0:T(8,128)(2,1)}, u32[]{:S(2)}, u32[]{:S(2)}) collective-permute-start(bf16[3,96,768]{2,1,0:T(8,128)(2,1)} %get-tuple-element.175), channel_id=1, source_target_pairs={{0,8},{4,12},{8,0},{12,4},{16,24},{20,28},{24,16},{28,20},{1,9},{5... | collective-permute-start | bytes 1327112 | tf_op jit(solution)/shard_map/ppermute | solution.py:386
  75.4 19.7 %collective-permute-start.4 = (bf16[3,96,768]{2,1,0:T(8,128)(2,1)}, bf16[3,96,768]{2,1,0:T(8,128)(2,1)}, u32[]{:S(2)}, u32[]{:S(2)}) collective-permute-start(bf16[3,96,768]{2,1,0:T(8,128)(2,1)} %get-tuple-element.175), channel_id=1, source_target_pairs={{0,16},{4,20},{8,24},{12,28},{16,0},{20,4},{24,8},{28,12},{1,17},{... | collective-permute-start | bytes 1327112 | tf_op jit(solution)/shard_map/ppermute | solution.py:386
  76.9 18.1 %collective-permute-start.5 = (bf16[3,96,768]{2,1,0:T(8,128)(2,1)}, bf16[3,96,768]{2,1,0:T(8,128)(2,1)}, u32[]{:S(2)}, u32[]{:S(2)}) collective-permute-start(bf16[3,96,768]{2,1,0:T(8,128)(2,1)} %get-tuple-element.175), channel_id=1, source_target_pairs={{0,24},{4,28},{8,16},{12,20},{16,8},{20,12},{24,0},{28,4},{1,25},{... | collective-permute-start | bytes 1327112 | tf_op jit(solution)/shard_map/ppermute | solution.py:386
  86.0 12.7 %collective-permute-start.6 = (bf16[3,96,768]{2,1,0:T(8,128)(2,1)}, bf16[3,96,768]{2,1,0:T(8,128)(2,1)S(1)}, u32[]{:S(2)}, u32[]{:S(2)}) collective-permute-start(bf16[3,96,768]{2,1,0:T(8,128)(2,1)} %get-tuple-element.175), channel_id=1, source_target_pairs={{0,4},{4,0},{8,12},{12,8},{16,20},{20,16},{24,28},{28,24},{1,5},{5... | collective-permute-start | bytes 1327112 | tf_op jit(solution)/shard_map/ppermute | solution.py:388
  91.8 22.5 %collective-permute-start.16 = (bf16[3,96,1536]{2,1,0:T(8,128)(2,1)S(1)}, bf16[3,96,1536]{2,1,0:T(8,128)(2,1)S(1)}, u32[]{:S(2)}, u32[]{:S(2)}) collective-permute-start(bf16[3,96,1536]{2,1,0:T(8,128)(2,1)S(1)} %get-tuple-element.168), channel_id=1, source_target_pairs={{0,8},{4,12},{8,0},{12,4},{16,24},{20,28},{24,16},{28,20},{1,9},{5... | collective-permute-start | bytes 2654216 | tf_op jit(solution)/shard_map/ppermute | solution.py:386
  93.2 7.1 %collective-permute-start.7 = (bf16[3,96,768]{2,1,0:T(8,128)(2,1)}, bf16[3,96,768]{2,1,0:T(8,128)(2,1)S(1)}, u32[]{:S(2)}, u32[]{:S(2)}) collective-permute-start(bf16[3,96,768]{2,1,0:T(8,128)(2,1)} %collective-permute-done.3), channel_id=1, source_target_pairs={{0,4},{4,0},{8,12},{12,8},{16,20},{20,16},{24,28},{28,24},{1,5},{5... | collective-permute-start | bytes 1327112 | tf_op jit(solution)/shard_map/ppermute | solution.py:388
  95.0 6.1 %collective-permute-start.8 = (bf16[3,96,768]{2,1,0:T(8,128)(2,1)}, bf16[3,96,768]{2,1,0:T(8,128)(2,1)S(1)}, u32[]{:S(2)}, u32[]{:S(2)}) collective-permute-start(bf16[3,96,768]{2,1,0:T(8,128)(2,1)} %collective-permute-done.4), channel_id=1, source_target_pairs={{0,4},{4,0},{8,12},{12,8},{16,20},{20,16},{24,28},{28,24},{1,5},{5... | collective-permute-start | bytes 1327112 | tf_op jit(solution)/shard_map/ppermute | solution.py:388
  95.0 6.2 %collective-permute-start.9 = (bf16[3,96,768]{2,1,0:T(8,128)(2,1)}, bf16[3,96,768]{2,1,0:T(8,128)(2,1)S(1)}, u32[]{:S(2)}, u32[]{:S(2)}) collective-permute-start(bf16[3,96,768]{2,1,0:T(8,128)(2,1)} %collective-permute-done.5), channel_id=1, source_target_pairs={{0,4},{4,0},{8,12},{12,8},{16,20},{20,16},{24,28},{28,24},{1,5},{5... | collective-permute-start | bytes 1327112 | tf_op jit(solution)/shard_map/ppermute | solution.py:388
  98.7 40.6 %collective-permute-start.17 = (bf16[3,96,1536]{2,1,0:T(8,128)(2,1)S(1)}, bf16[3,96,1536]{2,1,0:T(8,128)(2,1)S(1)}, u32[]{:S(2)}, u32[]{:S(2)}) collective-permute-start(bf16[3,96,1536]{2,1,0:T(8,128)(2,1)S(1)} %get-tuple-element.168), channel_id=1, source_target_pairs={{0,16},{4,20},{8,24},{12,28},{16,0},{20,4},{24,8},{28,12},{1,17},{... | collective-permute-start | bytes 2654216 | tf_op jit(solution)/shard_map/ppermute | solution.py:386
  100.3 40.0 %collective-permute-start.18 = (bf16[3,96,1536]{2,1,0:T(8,128)(2,1)S(1)}, bf16[3,96,1536]{2,1,0:T(8,128)(2,1)}, u32[]{:S(2)}, u32[]{:S(2)}) collective-permute-start(bf16[3,96,1536]{2,1,0:T(8,128)(2,1)S(1)} %get-tuple-element.168), channel_id=1, source_target_pairs={{0,24},{4,28},{8,16},{12,20},{16,8},{20,12},{24,0},{28,4},{1,25},{... | collective-permute-start | bytes 2654216 | tf_op jit(solution)/shard_map/ppermute | solution.py:386
  101.1 41.8 %collective-permute-start.19 = (bf16[3,96,1536]{2,1,0:T(8,128)(2,1)S(1)}, bf16[3,96,1536]{2,1,0:T(8,128)(2,1)S(1)}, u32[]{:S(2)}, u32[]{:S(2)}) collective-permute-start(bf16[3,96,1536]{2,1,0:T(8,128)(2,1)S(1)} %get-tuple-element.168), channel_id=1, source_target_pairs={{0,4},{4,0},{8,12},{12,8},{16,20},{20,16},{24,28},{28,24},{1,5},{5... | collective-permute-start | bytes 2654216 | tf_op jit(solution)/shard_map/ppermute | solution.py:388
  114.2 29.8 %collective-permute-start.20 = (bf16[3,96,1536]{2,1,0:T(8,128)(2,1)S(1)}, bf16[3,96,1536]{2,1,0:T(8,128)(2,1)S(1)}, u32[]{:S(2)}, u32[]{:S(2)}) collective-permute-start(bf16[3,96,1536]{2,1,0:T(8,128)(2,1)S(1)} %collective-permute-done.16), channel_id=1, source_target_pairs={{0,4},{4,0},{8,12},{12,8},{16,20},{20,16},{24,28},{28,24},{1,5},{5... | collective-permute-start | bytes 2654216 | tf_op jit(solution)/shard_map/ppermute | solution.py:388
  139.3 5.7 collective-permute-start.21
  140.3 12.4 %collective-permute-start.22 = (bf16[3,96,1536]{2,1,0:T(8,128)(2,1)}, bf16[3,96,1536]{2,1,0:T(8,128)(2,1)S(1)}, u32[]{:S(2)}, u32[]{:S(2)}) collective-permute-start(bf16[3,96,1536]{2,1,0:T(8,128)(2,1)} %collective-permute-done.18), channel_id=1, source_target_pairs={{0,4},{4,0},{8,12},{12,8},{16,20},{20,16},{24,28},{28,24},{1,5},{5... | collective-permute-start | bytes 2654216 | tf_op jit(solution)/shard_map/ppermute | solution.py:388
  146.0 58.8 %all-to-all-start.1 = ((bf16[4,256,768]{2,1,0:T(8,128)(2,1)}), bf16[4,256,768]{2,1,0:T(8,128)(2,1)}, u32[]{:S(2)}, u32[]{:S(2)}) async-start(bf16[4,256,768]{2,1,0:T(8,128)(2,1)} %param.29), calls=%async_computation.1 | async-start | bytes 3145728 | tf_op jit(solution)/shard_map/all_to_all | solution.py:423
  278.0 138.3 %collective-permute-start.30 = (bf16[4,4,96,1536]{3,2,0,1:T(8,128)(2,1)}, bf16[4,4,96,1536]{3,2,0,1:T(8,128)(2,1)}, u32[]{:S(2)}, u32[]{:S(2)}) collective-permute-start(bf16[4,4,96,1536]{3,2,0,1:T(8,128)(2,1)} %bitcast.141), channel_id=1, source_target_pairs={{0,4},{4,0},{8,12},{12,8},{16,20},{20,16},{24,28},{28,24},{1,5},{5... | collective-permute-start | bytes 14155784 | tf_op jit(solution)/shard_map/ppermute | solution.py:407
  363.1 43.0 %all-to-all-start.3 = ((bf16[4,2,98304]{2,1,0:T(2,128)(2,1)}), bf16[4,2,98304]{2,1,0:T(2,128)(2,1)}, u32[]{:S(2)}, u32[]{:S(2)}) async-start(bf16[4,2,98304]{2,1,0:T(2,128)(2,1)} %reshape.157), calls=%async_computation.3 | async-start | bytes 3145728 | tf_op jit(solution)/shard_map/all_to_all | solution.py:427
  372.9 37.7 %collective-permute-start.23 = (bf16[4,4,96,768]{3,2,1,0:T(8,128)(2,1)}, bf16[4,4,96,768]{3,2,1,0:T(8,128)(2,1)}, u32[]{:S(2)}, u32[]{:S(2)}) collective-permute-start(bf16[4,4,96,768]{3,2,1,0:T(8,128)(2,1)} %dynamic-slice_bitcast_fusion), channel_id=1, source_target_pairs={{0,4},{4,0},{8,12},{12,8},{16,20},{20,16},{24,28},{28,24},{1,5},{5... | collective-permute-start | bytes 7077896 | tf_op jit(solution)/shard_map/ppermute | solution.py:407
  406.1 138.8 %all-to-all-start.2 = ((bf16[4,2,98304]{2,1,0:T(2,128)(2,1)}), bf16[4,2,98304]{2,1,0:T(2,128)(2,1)}, u32[]{:S(2)}, u32[]{:S(2)}) async-start(bf16[4,2,98304]{2,1,0:T(2,128)(2,1)} %reshape.155), calls=%async_computation.2 | async-start | bytes 3145728 | tf_op jit(solution)/shard_map/all_to_all | solution.py:427
  415.1 16.4 %collective-permute-start.24 = (bf16[4,96,768]{2,1,0:T(8,128)(2,1)S(1)}, bf16[4,96,768]{2,1,0:T(8,128)(2,1)}, u32[]{:S(2)}, u32[]{:S(2)}) collective-permute-start(bf16[4,96,768]{2,1,0:T(8,128)(2,1)S(1)} %get-tuple-element.162), channel_id=1, source_target_pairs={{0,8},{4,12},{8,0},{12,4},{16,24},{20,28},{24,16},{28,20},{1,9},{5... | collective-permute-start | bytes 1769480 | tf_op jit(solution)/shard_map/ppermute | solution.py:412
  420.2 14.0 %copy-start.22 = (f32[192,2]{1,0:T(8,128)S(1)}, f32[192,2]{1,0:T(8,128)}, u32[]{:S(2)}) copy-start(f32[192,2]{1,0:T(8,128)} %get-tuple-element.71) | copy-start | bytes 4612
  420.2 14.4 %copy-start.27 = (f32[4,1,768]{2,1,0:T(1,128)S(1)}, f32[4,1,768]{2,1,0:T(1,128)}, u32[]{:S(2)}) copy-start(f32[4,1,768]{2,1,0:T(1,128)} %get-tuple-element.72) | copy-start | bytes 36868
  423.4 130.1 %collective-permute-start.31 = (bf16[4,96,1536]{2,1,0:T(8,128)(2,1)}, bf16[4,96,1536]{2,1,0:T(8,128)(2,1)}, u32[]{:S(2)}, u32[]{:S(2)}) collective-permute-start(bf16[4,96,1536]{2,1,0:T(8,128)(2,1)} %get-tuple-element.156), channel_id=1, source_target_pairs={{0,8},{4,12},{8,0},{12,4},{16,24},{20,28},{24,16},{28,20},{1,9},{5... | collective-permute-start | bytes 3538952 | tf_op jit(solution)/shard_map/ppermute | solution.py:412
  424.2 131.0 %collective-permute-start.32 = (bf16[4,96,1536]{2,1,0:T(8,128)(2,1)}, bf16[4,96,1536]{2,1,0:T(8,128)(2,1)}, u32[]{:S(2)}, u32[]{:S(2)}) collective-permute-start(bf16[4,96,1536]{2,1,0:T(8,128)(2,1)} %get-tuple-element.158), channel_id=1, source_target_pairs={{0,16},{4,20},{8,24},{12,28},{16,0},{20,4},{24,8},{28,12},{1,17},{... | collective-permute-start | bytes 3538952 | tf_op jit(solution)/shard_map/ppermute | solution.py:412
  425.7 129.4 %collective-permute-start.33 = (bf16[4,96,1536]{2,1,0:T(8,128)(2,1)}, bf16[4,96,1536]{2,1,0:T(8,128)(2,1)}, u32[]{:S(2)}, u32[]{:S(2)}) collective-permute-start(bf16[4,96,1536]{2,1,0:T(8,128)(2,1)} %get-tuple-element.157), channel_id=1, source_target_pairs={{0,24},{4,28},{8,16},{12,20},{16,8},{20,12},{24,0},{28,4},{1,25},{... | collective-permute-start | bytes 3538952 | tf_op jit(solution)/shard_map/ppermute | solution.py:412
  426.9 122.5 %collective-permute-start.25 = (bf16[4,96,768]{2,1,0:T(8,128)(2,1)}, bf16[4,96,768]{2,1,0:T(8,128)(2,1)}, u32[]{:S(2)}, u32[]{:S(2)}) collective-permute-start(bf16[4,96,768]{2,1,0:T(8,128)(2,1)} %get-tuple-element.164), channel_id=1, source_target_pairs={{0,16},{4,20},{8,24},{12,28},{16,0},{20,4},{24,8},{28,12},{1,17},{... | collective-permute-start | bytes 1769480 | tf_op jit(solution)/shard_map/ppermute | solution.py:412
  431.5 117.9 %collective-permute-start.26 = (bf16[4,96,768]{2,1,0:T(8,128)(2,1)}, bf16[4,96,768]{2,1,0:T(8,128)(2,1)}, u32[]{:S(2)}, u32[]{:S(2)}) collective-permute-start(bf16[4,96,768]{2,1,0:T(8,128)(2,1)} %get-tuple-element.163), channel_id=1, source_target_pairs={{0,24},{4,28},{8,16},{12,20},{16,8},{20,12},{24,0},{28,4},{1,25},{... | collective-permute-start | bytes 1769480 | tf_op jit(solution)/shard_map/ppermute | solution.py:412
  551.3 9.1 %collective-permute-start.27 = (bf16[96,768]{1,0:T(8,128)(2,1)S(1)}, bf16[96,768]{1,0:T(8,128)(2,1)S(1)}, u32[]{:S(2)}, u32[]{:S(2)}) collective-permute-start(bf16[96,768]{1,0:T(8,128)(2,1)S(1)} %get-tuple-element.172), channel_id=1, source_target_pairs={{0,1},{1,2},{2,3},{3,0},{4,5},{5,6},{6,7},{7,4},{8,9},{9,10},{10,1... | collective-permute-start | bytes 442376 | tf_op jit(solution)/shard_map/ppermute | solution.py:416
  551.8 23.6 %collective-permute-start.28 = (bf16[96,768]{1,0:T(8,128)(2,1)S(1)}, bf16[96,768]{1,0:T(8,128)(2,1)S(1)}, u32[]{:S(2)}, u32[]{:S(2)}) collective-permute-start(bf16[96,768]{1,0:T(8,128)(2,1)S(1)} %get-tuple-element.174), channel_id=1, source_target_pairs={{0,2},{1,3},{2,0},{3,1},{4,6},{5,7},{6,4},{7,5},{8,10},{9,11},{10,... | collective-permute-start | bytes 442376 | tf_op jit(solution)/shard_map/ppermute | solution.py:416
  553.4 22.0 %collective-permute-start.29 = (bf16[96,768]{1,0:T(8,128)(2,1)S(1)}, bf16[96,768]{1,0:T(8,128)(2,1)S(1)}, u32[]{:S(2)}, u32[]{:S(2)}) collective-permute-start(bf16[96,768]{1,0:T(8,128)(2,1)S(1)} %get-tuple-element.173), channel_id=1, source_target_pairs={{0,3},{1,0},{2,1},{3,2},{4,7},{5,4},{6,5},{7,6},{8,11},{9,8},{10,9... | collective-permute-start | bytes 442376 | tf_op jit(solution)/shard_map/ppermute | solution.py:416
  558.2 19.2 %collective-permute-start.34 = (bf16[96,1536]{1,0:T(8,128)(2,1)S(1)}, bf16[96,1536]{1,0:T(8,128)(2,1)S(1)}, u32[]{:S(2)}, u32[]{:S(2)}) collective-permute-start(bf16[96,1536]{1,0:T(8,128)(2,1)S(1)} %get-tuple-element.165), channel_id=1, source_target_pairs={{0,1},{1,2},{2,3},{3,0},{4,5},{5,6},{6,7},{7,4},{8,9},{9,10},{10,1... | collective-permute-start | bytes 884744 | tf_op jit(solution)/shard_map/ppermute | solution.py:416
  558.8 27.8 %collective-permute-start.35 = (bf16[96,1536]{1,0:T(8,128)(2,1)S(1)}, bf16[96,1536]{1,0:T(8,128)(2,1)S(1)}, u32[]{:S(2)}, u32[]{:S(2)}) collective-permute-start(bf16[96,1536]{1,0:T(8,128)(2,1)S(1)} %get-tuple-element.167), channel_id=1, source_target_pairs={{0,2},{1,3},{2,0},{3,1},{4,6},{5,7},{6,4},{7,5},{8,10},{9,11},{10,... | collective-permute-start | bytes 884744 | tf_op jit(solution)/shard_map/ppermute | solution.py:416
  560.3 26.3 %collective-permute-start.36 = (bf16[96,1536]{1,0:T(8,128)(2,1)S(1)}, bf16[96,1536]{1,0:T(8,128)(2,1)}, u32[]{:S(2)}, u32[]{:S(2)}) collective-permute-start(bf16[96,1536]{1,0:T(8,128)(2,1)S(1)} %get-tuple-element.166), channel_id=1, source_target_pairs={{0,3},{1,0},{2,1},{3,2},{4,7},{5,4},{6,5},{7,6},{8,11},{9,8},{10,9... | collective-permute-start | bytes 884744 | tf_op jit(solution)/shard_map/ppermute | solution.py:416
  (32 other events, 234.3 us)

commit v2 on v0

v2 whole, which is shorter than its diff:
```python
import functools

import jax
import jax.numpy as jnp
from jax import lax
from jax.experimental import pallas as pl
from jax.experimental.pallas import tpu as pltpu
from jax.sharding import PartitionSpec as P

BF = jnp.bfloat16
F32 = jnp.float32
HEAD = 64
EPS = 1e-05
GELU_C = 0.7978845608028654
GELU_A = 0.044715
BLOCK = 256
MIB = 1024 * 1024
KEEP = (0, 2, 4, 6)
PAIR = 1


def dot(lhs, rhs, lhs_dim, rhs_dim):
    return lax.dot_general(
        lhs, rhs, (((lhs_dim,), (rhs_dim,)), ((), ())), preferred_element_type=F32
    )


def normalize(value):
    mean = jnp.mean(value, axis=-1, keepdims=True)
    centred = value - mean
    variance = jnp.mean(centred * centred, axis=-1, keepdims=True)
    rstd = lax.rsqrt(variance + EPS)
    return centred * rstd, rstd


def norm_backward(grad, xhat, rstd, gain):
    scaled = grad * gain
    mean_e = jnp.mean(scaled, axis=-1, keepdims=True)
    mean_ex = jnp.mean(scaled * xhat, axis=-1, keepdims=True)
    return rstd * (scaled - mean_e - xhat * mean_ex)


def column(line):
    return jnp.broadcast_to(line, (8, line.shape[1])).T[:, 0:1]


def block_rows(index, size=BLOCK):
    return pl.ds(pl.multiple_of(index * size, size), size)


VMEM = pl.BlockSpec(memory_space=pltpu.VMEM)
SMEM = pl.BlockSpec(memory_space=pltpu.SMEM)
HBM = pl.BlockSpec(memory_space=pl.ANY)


def call(kernel, name, outs, specs, args, out_specs=None, vmem=60, scratch=(), grid=()):
    shapes = tuple(jax.ShapeDtypeStruct(*o) for o in outs)
    return pl.pallas_call(
        kernel,
        grid=grid,
        out_shape=shapes,
        in_specs=specs,
        out_specs=out_specs or (VMEM,) * len(outs),
        scratch_shapes=list(scratch),
        compiler_params=pltpu.CompilerParams(vmem_limit_bytes=vmem * MIB),
        name=name,
        cost_estimate=pl.CostEstimate(flops=1, bytes_accessed=1, transcendentals=0),
    )(*args)


def fixed(shape):
    return pl.BlockSpec(shape, lambda *_: (0,) * len(shape), pipeline_mode=pl.Buffered(1))


def nth(shape, base=0):
    return pl.BlockSpec((1,) + tuple(shape[1:]), lambda t: (lax.rem(t + base, shape[0]),) + (0,) * (len(shape) - 1))


def own_copies(owns, wholes, sems):
    return [
        pltpu.make_async_copy(own, whole.at[0], sems.at[0, i]) for i, (own, whole) in enumerate(zip(owns, wholes))
    ]


def piece_copies(ids_ref, sources, plan, wholes, sems, k, slot):
    copies = []
    for src, (place, arrays) in zip(sources, plan):
        rows = src.shape[3]
        for m in range(src.shape[0]):
            at = pl.multiple_of(ids_ref[place + m] * rows, rows)
            for u, array in enumerate(arrays):
                copies.append(
                    pltpu.make_async_copy(
                        src.at[m, k - 1, u], wholes[array].at[slot, pl.ds(at, rows), :], sems.at[slot, len(copies)]
                    )
                )
    return copies


def piece_count(sources):
    return sum(src.shape[0] * src.shape[2] for src in sources)


def fetch(base, count, step, ids_ref, owns, sources, plan, wholes, sems):
    slot = lax.rem(step, 2)
    begins_own = base == 0

    def start():
        @pl.when(step == 0)
        def _():
            for copy in own_copies(owns, wholes, sems) if begins_own else piece_copies(
                ids_ref, sources, plan, wholes, sems, base, 0
            ):
                copy.start()

        @pl.when(step < count - 1)
        def _():
            for copy in piece_copies(ids_ref, sources, plan, wholes, sems, base + step + 1, lax.rem(step + 1, 2)):
                copy.start()

    def wait():
        if begins_own:
            @pl.when(step == 0)
            def _():
                for copy in own_copies(owns, wholes, sems):
                    copy.wait()

        @pl.when(step > 0 if begins_own else step >= 0)
        def _():
            for copy in piece_copies(ids_ref, sources, plan, wholes, sems, base + step, slot):
                copy.wait()

    return start, wait


def first_kernel(gain_ref, bias_ref, x_ref, n1t_ref):
    xhat, _ = normalize(x_ref[...].astype(F32))
    n1t_ref[...] = (xhat * gain_ref[...] + bias_ref[...]).T.astype(BF)


def first(gain, bias, x):
    seq, width = x.shape
    return call(
        first_kernel,
        "first",
        [((width, seq), BF)],
        [fixed(gain.shape), fixed(bias.shape), pl.BlockSpec((BLOCK, width), lambda i: (i, 0))],
        (gain, bias, x),
        out_specs=(pl.BlockSpec((width, BLOCK), lambda i: (0, i)),),
        grid=(seq // BLOCK,),
    )[0]


def mask_bias(docs_ref, mask_ref):
    seq = mask_ref.shape[0]
    docs = docs_ref[...]
    docs_col = column(docs)
    for begin in range(0, seq, BLOCK):
        end = begin + BLOCK
        same = docs_col[0:end] == docs[:, begin:end]
        place_k = lax.broadcasted_iota(jnp.int32, (end, BLOCK), 0)
        place_q = begin + lax.broadcasted_iota(jnp.int32, (end, BLOCK), 1)
        allowed = same & (place_k <= place_q)
        mask_ref[0:end, begin:end] = jnp.where(allowed, 0.0, -1e30).astype(F32)


def attend_kernel(base, plan, ids_ref, n1t_ref, small_ref, docs_ref, own_ref, *refs):
    sources, (qkvt_ref, at_ref, lse_ref, a_ref, mask_ref, held_ref, sems) = refs[: len(plan)], refs[len(plan) :]
    step = pl.program_id(0)
    start, wait = fetch(base, pl.num_programs(0), step, ids_ref, [own_ref], sources, plan, [held_ref], sems)
    start()
    seq = n1t_ref.shape[1]
    part = at_ref.shape[1]

    @pl.when(pl.program_id(0) == 0)
    def _():
        mask_bias(docs_ref, mask_ref)

    wait()
    a_ref[0] = held_ref[lax.rem(step, 2)]
    proj = dot(a_ref[0, 0 : 3 * part, :], n1t_ref[...], 1, 0)
    qkvt_ref[0, 0:part, :] = (proj[0:part] + column(small_ref[0, 0:1, 0:part])).astype(BF)
    qkvt_ref[0, part : 2 * part, :] = proj[part : 2 * part].astype(BF)
    qkvt_ref[0, 2 * part :, :] = (proj[2 * part :] + column(small_ref[0, 1:2, 0:part])).astype(BF)
    for h in range(part // HEAD):
        q_rows = slice(h * HEAD, (h + 1) * HEAD)
        k_rows = slice(part + h * HEAD, part + (h + 1) * HEAD)
        v_rows = slice(2 * part + h * HEAD, 2 * part + (h + 1) * HEAD)
        keys = qkvt_ref[0, k_rows, :].T
        for begin in range(0, seq, BLOCK):
            end = begin + BLOCK
            q_blk = qkvt_ref[0, q_rows, begin:end] * BF(0.125)
            scores = dot(keys[0:end], q_blk, 1, 0) + mask_ref[0:end, begin:end]
            top = jnp.max(scores, axis=0, keepdims=True)
            expo = jnp.exp(scores - top)
            total = jnp.sum(expo, axis=0, keepdims=True)
            out = dot(qkvt_ref[0, v_rows, 0:end], expo.astype(BF), 1, 0)
            at_ref[0, q_rows, begin:end] = (out / total).astype(BF)
            lse_ref[0, h : h + 1, begin:end] = top + jnp.log(total)


def attend(group, ids, n1t, own_a, sources, plan, smalls, docs):
    width, seq = n1t.shape
    base, count, part = group[0], len(group), own_a.shape[0] // 4
    shapes = [(count, 3 * part, seq), (count, part, seq), (count, 8, seq), (count,) + own_a.shape]
    return call(
        functools.partial(attend_kernel, base, plan),
        "attend",
        [(shapes[0], BF), (shapes[1], BF), (shapes[2], F32), (shapes[3], BF)],
        [SMEM, fixed(n1t.shape), nth(smalls.shape, base), fixed(docs.shape)] + [HBM] * (1 + len(sources)),
        (ids, n1t, smalls, docs, own_a) + tuple(sources),
        out_specs=tuple(nth(s) for s in shapes),
        grid=(count,),
        scratch=[
            pltpu.VMEM((seq, seq), F32),
            pltpu.VMEM((2,) + own_a.shape, BF),
            pltpu.SemaphoreType.DMA((2, piece_count(sources))),
        ],
    )


def split_rows(whole_ref, ids_ref, outs, array=0):
    for g, out in enumerate(outs):
        count, rows = out.shape[0], out.shape[3]
        for m in range(count):
            at = pl.multiple_of(ids_ref[g * count + m] * rows, rows)
            out[m, 0, array] = whole_ref[pl.ds(at, rows), :]


def attend_back_kernel(
    n_split, ids_ref, gmt_ref, n1t_ref, a_ref, qkvt_ref, at_ref, lse_ref, docs_ref, gpt_ref, gb_ref, *refs
):
    splits, (mask_ref, gat_ref, dkv_ref, da_ref) = refs[:n_split], refs[n_split:]
    seq = n1t_ref.shape[1]
    part = at_ref.shape[1]

    @pl.when(pl.program_id(0) == 0)
    def _():
        mask_bias(docs_ref, mask_ref)

    gat_ref[...] = dot(a_ref[0, 3 * part :, :], gmt_ref[...], 1, 0).astype(BF)
    for h in range(part // HEAD):
        q_rows = slice(h * HEAD, (h + 1) * HEAD)
        k_rows = slice(part + h * HEAD, part + (h + 1) * HEAD)
        v_rows = slice(2 * part + h * HEAD, 2 * part + (h + 1) * HEAD)
        keys = qkvt_ref[0, k_rows, :].T
        values = qkvt_ref[0, v_rows, :].T
        for begin in range(0, seq, BLOCK):
            end = begin + BLOCK
            q_blk = qkvt_ref[0, q_rows, begin:end] * BF(0.125)
            g_blk = gat_ref[q_rows, begin:end]
            delta = jnp.sum(
                g_blk.astype(F32) * at_ref[0, q_rows, begin:end].astype(F32), axis=0, keepdims=True
            )
            scores = dot(keys[0:end], q_blk, 1, 0) + mask_ref[0:end, begin:end]
            probs = jnp.exp(scores - lse_ref[0, h : h + 1, begin:end])
            grad_probs = dot(values[0:end], g_blk, 1, 0)
            probs_low = probs.astype(BF)
            grad_scores = (probs * (grad_probs - delta)).astype(BF)
            gpt_ref[0, q_rows, begin:end] = (
                0.125 * dot(qkvt_ref[0, k_rows, 0:end], grad_scores, 1, 0)
            ).astype(BF)
            gk = dot(q_blk, grad_scores, 1, 1)
            gv = dot(g_blk, probs_low, 1, 1)
            if begin > 0:
                dkv_ref[0:HEAD, 0:begin] += gk[:, 0:begin]
                dkv_ref[HEAD:, 0:begin] += gv[:, 0:begin]
            dkv_ref[0:HEAD, begin:end] = gk[:, begin:end]
            dkv_ref[HEAD:, begin:end] = gv[:, begin:end]
        gpt_ref[0, k_rows, :] = dkv_ref[0:HEAD, :].astype(BF)
        gpt_ref[0, v_rows, :] = dkv_ref[HEAD:, :].astype(BF)
    ones = jnp.ones((8, seq), BF)
    gb_ref[0, 0:1, :] = dot(ones, gpt_ref[0, 0:part, :], 1, 1)[0:1]
    gb_ref[0, 1:2, :] = dot(ones, gpt_ref[0, 2 * part : 3 * part, :], 1, 1)[0:1]
    da_ref[:, 0 : 3 * part] = dot(n1t_ref[...], gpt_ref[0], 1, 1).astype(BF)
    da_ref[:, 3 * part :] = dot(gmt_ref[...], at_ref[0], 1, 1).astype(BF)
    split_rows(da_ref, ids_ref, splits)


def attend_back(splits, ids, gmt, n1t, qkvt, at, lse, a_part, docs):
    width, seq = n1t.shape
    part = at.shape[1]
    n_split, blocks = splits
    count = at.shape[0]
    cut = (blocks, count, 1, width // (n_split * blocks), 4 * part)
    cut_spec = pl.BlockSpec((blocks, 1) + cut[2:], lambda t: (0, t, 0, 0, 0))
    return call(
        functools.partial(attend_back_kernel, n_split),
        "attend_back",
        [((count, 3 * part, seq), BF), ((count, 2, part), F32)] + [(cut, BF)] * n_split,
        [SMEM, fixed(gmt.shape), fixed(n1t.shape), nth(a_part.shape), nth(qkvt.shape), nth(at.shape),
         nth(lse.shape), fixed(docs.shape)],
        (ids, gmt, n1t, a_part, qkvt, at, lse, docs),
        out_specs=(nth((count, 3 * part, seq)), nth((count, 2, part))) + (cut_spec,) * n_split,
        grid=(count,),
        scratch=[
            pltpu.VMEM((seq, seq), F32),
            pltpu.VMEM((part, seq), BF),
            pltpu.VMEM((2 * HEAD, seq), F32),
            pltpu.VMEM((width, 4 * part), BF),
        ],
    )


def mlp_kernel(
    n_t, n_split, plan, ids_ref, x_ref, at_one_ref, at_two_ref, out_one_ref, out_two_ref, small_ref,
    out_bias_ref, gain_ref, bias_ref, down_bias_ref, own_up_ref, own_down_ref, *refs
):
    sources, refs = refs[: len(plan)], refs[len(plan) :]
    cot_ref, out_ref, *refs = refs
    gm_ref, gmt_ref, gvec_ref, gbup_ref = refs[:4]
    splits = refs[4 : 4 + n_split]
    (mixed_ref, n2_ref, n2t_ref, cott_ref, total_ref, grad_ref, act_ref, gpre_ref, dm_ref,
     up_all_ref, down_all_ref, sems) = refs[4 + n_split :]
    seq, width = x_ref.shape
    step_t = pl.program_id(0)
    blocks = seq // BLOCK
    slot = lax.rem(step_t, 2)
    wholes = [up_all_ref, down_all_ref]
    start, wait = fetch(0, n_t, step_t, ids_ref, [own_up_ref, own_down_ref], sources, plan, wholes, sems)
    up_ref, down_ref = up_all_ref.at[slot], down_all_ref.at[slot]
    start()

    @pl.when(step_t == 0)
    def _():
        gvec_ref[...] = jnp.zeros_like(gvec_ref)

        @pl.loop(0, blocks)
        def _(step):
            rows = block_rows(step)
            total = x_ref[rows, :].astype(F32) + out_bias_ref[...]
            for at_ref, w_out_ref in ((at_one_ref, out_one_ref), (at_two_ref, out_two_ref)):
                for t in range(at_ref.shape[0]):
                    total += dot(at_ref[t, :, rows].T, w_out_ref[t], 1, 0)
            mixed_ref[rows, :] = total
            xhat, _ = normalize(total)
            normed = (xhat * gain_ref[...] + bias_ref[...]).astype(BF)
            n2_ref[rows, :] = normed
            n2t_ref[:, rows] = normed.T
            held = cot_ref[rows, :]
            cott_ref[:, rows] = held.T
            gvec_ref[3:4, :] += jnp.sum(held.astype(F32), axis=0, keepdims=True)
            total_ref[rows, :] = jnp.zeros((BLOCK, width), F32)
            grad_ref[rows, :] = jnp.zeros((BLOCK, width), F32)

    wait()
    bias = small_ref[0, 2:3, :]

    def one(step, sums):
        rows = block_rows(step)
        pre = dot(n2_ref[rows, :], up_ref[...], 1, 0) + bias
        grad_act = dot(cot_ref[rows, :], down_ref[...], 1, 1)
        square = pre * pre
        curve = jnp.tanh(pre * (GELU_C + (GELU_C * GELU_A) * square))
        half = 0.5 + 0.5 * curve
        act = (pre * half).astype(BF)
        slope = half + (half - half * curve) * pre * (GELU_C + (3 * GELU_C * GELU_A) * square)
        grad_pre = (slope * grad_act).astype(BF)
        act_ref[rows, :] = act
        gpre_ref[rows, :] = grad_pre
        total_ref[rows, :] += dot(act, down_ref[...], 1, 0)
        grad_ref[rows, :] += dot(grad_pre, up_ref[...], 1, 1)
        return sums + jnp.sum(grad_pre.astype(F32), axis=0, keepdims=True)

    gbup_ref[0] = lax.fori_loop(0, blocks, one, jnp.zeros(bias.shape, F32), unroll=True)
    dm_ref[...] = dot(n2t_ref[...], gpre_ref[...], 1, 0).astype(BF)
    split_rows(dm_ref, ids_ref, splits, 0)
    dm_ref[...] = dot(cott_ref[...], act_ref[...], 1, 0).astype(BF)
    split_rows(dm_ref, ids_ref, splits, 1)

    @pl.when(step_t == n_t - 1)
    def _():
        @pl.loop(0, blocks)
        def _(step):
            rows = block_rows(step)
            xhat, rstd = normalize(mixed_ref[rows, :])
            grad_n = grad_ref[rows, :]
            grad_mixed = cot_ref[rows, :].astype(F32) + norm_backward(grad_n, xhat, rstd, gain_ref[...])
            gm_ref[rows, :] = grad_mixed
            gmt_ref[:, rows] = grad_mixed.T.astype(BF)
            gvec_ref[0:1, :] += jnp.sum(grad_mixed, axis=0, keepdims=True)
            gvec_ref[1:2, :] += jnp.sum(grad_n * xhat, axis=0, keepdims=True)
            gvec_ref[2:3, :] += jnp.sum(grad_n, axis=0, keepdims=True)
            out_ref[rows, :] = (mixed_ref[rows, :] + total_ref[rows, :] + down_bias_ref[...]).astype(BF)


def mlp(splits, ids, x, at_one, at_two, a_one, a_two, w_up, w_down, sources, plan, smalls, vecs, cot):
    seq, width = x.shape
    n_t, part = at_one.shape[0] + at_two.shape[0], at_one.shape[1]
    ff = w_up.shape[1]
    n_split, blocks = splits
    cut = (blocks, n_t, 2, width // (n_split * blocks), ff)
    cut_spec = pl.BlockSpec((blocks, 1) + cut[2:], lambda t: (0, t, 0, 0, 0))
    gbup = (n_t, 1, ff)
    return call(
        functools.partial(mlp_kernel, n_t, n_split, plan),
        "mlp",
        [((seq, width), BF), ((seq, width), F32), ((width, seq), BF), ((8, width), F32), (gbup, F32)]
        + [(cut, BF)] * n_split,
        [SMEM, fixed(x.shape), fixed(at_one.shape), fixed(at_two.shape),
         *[pl.BlockSpec((a.shape[0], part, width), lambda t: (0, 3, 0), pipeline_mode=pl.Buffered(1)) for a in (a_one, a_two)],
         nth(smalls.shape)] + [fixed((1, width))] * 4 + [HBM] * (2 + len(sources)) + [fixed(cot.shape)],
        (ids, x, at_one, at_two, a_one, a_two, smalls) + tuple(vecs) + (w_up, w_down) + tuple(sources) + (cot,),
        out_specs=(fixed((seq, width)), fixed((seq, width)), fixed((width, seq)), fixed((8, width)), nth(gbup))
        + (cut_spec,) * n_split,
        grid=(n_t,),
        scratch=[
            pltpu.VMEM((seq, width), F32),
            pltpu.VMEM((seq, width), BF),
            pltpu.VMEM((width, seq), BF),
            pltpu.VMEM((width, seq), BF),
            pltpu.VMEM((seq, width), F32),
            pltpu.VMEM((seq, width), F32),
            pltpu.VMEM((seq, ff), BF),
            pltpu.VMEM((seq, ff), BF),
            pltpu.VMEM((width, ff), BF),
            pltpu.VMEM((2, width, ff), BF),
            pltpu.VMEM((2, ff, width), BF),
            pltpu.SemaphoreType.DMA((2, max(2, piece_count(sources)))),
        ],
    )


def input_back_kernel(x_ref, gm_ref, gain_ref, a_one_ref, a_two_ref, one_ref, two_ref, out_ref, gvec_ref):

    @pl.when(pl.program_id(0) == 0)
    def _():
        gvec_ref[...] = jnp.zeros_like(gvec_ref)

    grad_n = None
    for gpt_ref, a_ref in ((one_ref, a_one_ref), (two_ref, a_two_ref)):
        for t in range(gpt_ref.shape[0]):
            share = dot(gpt_ref[t].T, a_ref[t], 1, 0)
            grad_n = share if grad_n is None else grad_n + share
    xhat, rstd = normalize(x_ref[...].astype(F32))
    out_ref[...] = (gm_ref[...] + norm_backward(grad_n, xhat, rstd, gain_ref[...])).astype(BF)
    gvec_ref[0:1, :] += jnp.sum(grad_n * xhat, axis=0, keepdims=True)
    gvec_ref[1:2, :] += jnp.sum(grad_n, axis=0, keepdims=True)


def input_back(x, gm, gain, a_one, a_two, one, two):
    seq, width = x.shape
    part3 = one.shape[1]
    by_rows = pl.BlockSpec((BLOCK, width), lambda i: (i, 0))

    def by_columns(gpt):
        return pl.BlockSpec(gpt.shape[:2] + (BLOCK,), lambda i: (0, 0, i))

    return call(
        input_back_kernel,
        "input_back",
        [((seq, width), BF), ((8, width), F32)],
        [by_rows, by_rows, fixed(gain.shape), fixed((one.shape[0], part3, width)), fixed((two.shape[0], part3, width)),
         by_columns(one), by_columns(two)],
        (x, gm, gain, a_one, a_two, one, two),
        out_specs=(by_rows, fixed((8, width))),
        grid=(seq // BLOCK,),
    )


def trade(value):
    return lax.all_to_all(value, "tensor", 0, 0, tiled=True)


def turn(value, by):
    return jnp.roll(value, -by, axis=0)


def swap(value, n_dp, mask):
    return lax.ppermute(value, "dp", [(i, i ^ mask) for i in range(n_dp)])


def after(value, *others):
    return lax.optimization_barrier((value,) + others)[0]


def chip_pieces(pieces, n_dp):
    if n_dp != 8:
        return [(lax.all_gather(pieces, "dp", axis=2, tiled=True), 0, tuple(range(pieces.shape[1])))]
    arrays = tuple(range(pieces.shape[1]))
    if len(arrays) == 1:
        return [(pieces, 0, arrays)] + [(swap(pieces, n_dp, mask), m + 1, arrays) for m, mask in enumerate(KEEP[1:])]
    by_x, by_y = swap(pieces, n_dp, KEEP[1]), swap(pieces, n_dp, KEEP[2])
    first_far = swap(by_y[:, 0:1], n_dp, KEEP[1])
    second_far = swap(by_x[:, 1:2], n_dp, KEEP[2])
    return [(pieces, 0, arrays), (by_x, 1, arrays), (by_y, 2, arrays), (first_far, 3, (0,)), (second_far, 3, (1,))]


def pair_pieces(mine, n_dp):
    if n_dp != 8:
        return [value[None] for value, _, _ in mine], tuple((place, arrays) for _, place, arrays in mine)
    both = mine + [(swap(value, n_dp, PAIR), place + len(KEEP), arrays) for value, place, arrays in mine]
    return [value[None] for value, _, _ in both], tuple((place, arrays) for _, place, arrays in both)


def pair_swap(parts, n_dp):
    return [swap(parts[1], n_dp, PAIR)] if n_dp == 8 else []


def pair_sum(parts, got, places, select):
    return [parts[0][p][select].astype(F32) + got[0][p][select].astype(F32) for p in places]


def chip_send(parts, got, n_dp, near, far, select):
    if n_dp != 8:
        whole = parts[0][0][select]
        return lax.psum_scatter(whole, "dp", scatter_dimension=whole.ndim - 2, tiled=True)
    return swap(jnp.stack(pair_sum(parts, got, (near, 3), select)).astype(BF), n_dp, KEEP[near])


def chip_pass(parts, got, sent, n_dp, near, far, select):
    if n_dp != 8:
        return [sent]
    here, there = pair_sum(parts, got, (0, far), select)
    here = here + sent[0].astype(F32)
    there = (there + sent[1].astype(F32)).astype(BF)
    return [here, swap(there, n_dp, KEEP[far])]


def chip_sum(terms):
    total = terms[0].astype(F32)
    for item in terms[1:]:
        total += item.astype(F32)
    return total


def in_parts(value):
    high = value.astype(BF)
    rest = value - high.astype(F32)
    middle = rest.astype(BF)
    return [high, middle, (rest - middle.astype(F32)).astype(BF)]


def small_vectors(b_qv, b_up):
    value = jnp.concatenate([jnp.pad(b_qv, ((0, 0), (0, b_up.shape[0] - b_qv.shape[1]))), b_up[None]])
    return jnp.concatenate(in_parts(value) + [jnp.zeros((7,) + b_up.shape, BF)])


def local(n_dp, n_t, inputs, doc_ids, ln1_gain, ln1_bias, w_qkv, b_qv, w_out, out_bias, ln2_gain, ln2_bias,
          w_up, b_up, w_down, down_bias, cotangent):
    width = inputs.shape[2]
    part, ff = w_out.shape[0], w_up.shape[1]
    dp = lax.axis_index("dp")
    tensor = lax.axis_index("tensor")
    own_rows = inputs.shape[0] // n_t
    rows = width // n_dp
    each_row = range(own_rows)
    splits = (2, 4) if n_dp == 8 else (1, 1)
    order = jnp.array(KEEP + tuple(m ^ PAIR for m in KEEP), jnp.int32)
    ids = order ^ dp if n_dp == 8 else jnp.zeros_like(order)
    half = n_t // 2
    groups = (tuple(range(half)), tuple(range(half, n_t)))

    def own_piece(whole):
        return lax.dynamic_slice_in_dim(whole, dp * rows, rows, 0)

    def others(gathered):
        return turn(gathered, tensor + 1)[: n_t - 1]

    def split_row(values):
        values = values.reshape((n_t, own_rows) + values.shape[1:])
        return [values[:, r].reshape(-1, width) for r in each_row]

    def join_row(values):
        blocks = jnp.stack([v.reshape(n_t, -1, width) for v in values], axis=1)
        return blocks.reshape((n_t * own_rows,) + blocks.shape[2:])

    own_a = jnp.concatenate([w_qkv.transpose(1, 2, 0).reshape(3 * part, width), w_out])
    pieces = jnp.concatenate([own_piece(own_a), own_piece(w_up), own_piece(w_down), small_vectors(b_qv, b_up)])
    gathered = trade(jnp.broadcast_to(pieces[None], (n_t,) + pieces.shape))
    smalls = turn(gathered[:, 3 * rows :].astype(F32), tensor)
    smalls = smalls[:, 0:3] + smalls[:, 3:6] + smalls[:, 6:9]
    stack_a, stack_m = others(gathered[:, :rows])[:, None], others(gathered[:, rows : 3 * rows])
    stack_m = stack_m.reshape(n_t - 1, 2, rows, width)
    mine_a = chip_pieces(stack_a, n_dp)
    x_rows = split_row(trade(after(inputs, gathered)))
    mine_m = chip_pieces(after(stack_m, [m[0] for m in mine_a]), n_dp)
    sources_a, plan_a = pair_pieces(mine_a, n_dp)
    cot_rows = split_row(trade(after(cotangent, x_rows)))
    vecs = [v[None] for v in (out_bias, ln2_gain, ln2_bias, down_bias)]
    doc_rows = lax.dynamic_slice_in_dim(doc_ids, tensor * own_rows, own_rows, 0)
    docs = [doc_rows[r : r + 1] for r in each_row]

    def total_of(*items):
        if len(items) == 1:
            return items[0]
        return sum(item.astype(F32) for item in items).astype(items[0].dtype)

    def together(results):
        return [jax.tree.map(total_of, *items) for items in zip(*results)]

    n1ts = [first(ln1_gain[None], ln1_bias[None], x) for x in x_rows]
    seen_one = [attend(groups[0], ids, n1ts[r], own_a, sources_a, plan_a, smalls, docs[r]) for r in each_row]
    n1ts, values_m = lax.optimization_barrier((n1ts, [m[0] for m in mine_m], seen_one))[:2]
    mine_m = [(value,) + m[1:] for value, m in zip(values_m, mine_m)]
    sources_m, plan_m = pair_pieces(mine_m, n_dp)
    seen_two = [attend(groups[1], ids, n1ts[r], own_a, sources_a, plan_a, smalls, docs[r]) for r in each_row]
    sources_m, cot_rows = lax.optimization_barrier((sources_m, cot_rows, seen_two))[:2]
    made = [
        mlp(splits, ids, x_rows[r], seen_one[r][1], seen_two[r][1], seen_one[r][3], seen_two[r][3], w_up, w_down,
            sources_m, plan_m, smalls, vecs, cot_rows[r])
        for r in each_row
    ]
    gvec, gbup, *dms = together([m[3:] for m in made])
    got_m = pair_swap(dms, n_dp)
    block_out = trade(join_row([m[0] for m in made]))

    def back(gmts, seen):
        items = [attend_back(splits, ids, gmts[r], n1ts[r], *seen[r], docs[r]) for r in each_row]
        return [i[0] for i in items], together([i[1:] for i in items])

    up_way, down_way = (1, 2, (slice(None), 0)), (2, 1, (slice(None), 1))
    one_way, two_way = (1, 2, ()), (2, 1, ())
    gmts = [m[2] for m in made]
    gpt_two, (gb_two, *da_two) = back(gmts, seen_two)
    got_m, dms = lax.optimization_barrier((got_m, dms, gpt_two))[:2]
    sent_m = [chip_send(dms, got_m, n_dp, *way) for way in (up_way, down_way)]
    got_two = pair_swap(da_two, n_dp)
    gmts, dms, got_m = lax.optimization_barrier((gmts, dms, got_m, gpt_two))[:3]
    gpt_one, (gb_one, *da_one) = back(gmts, seen_one)
    got_one = pair_swap(da_one, n_dp)
    block_out, got_two, sent_m, dms, got_m = lax.optimization_barrier(
        (block_out, got_two, sent_m, dms, got_m, gpt_one)
    )[:5]
    passed_m = [chip_pass(dms, got_m, sent, n_dp, *way) for sent, way in zip(sent_m, (up_way, down_way))]
    gms = lax.optimization_barrier(([m[1] for m in made], gpt_one, block_out, sent_m))[0]
    ends = [
        input_back(x_rows[r], gms[r], ln1_gain[None], seen_two[r][3], seen_one[r][3], gpt_two[r], gpt_one[r])
        for r in each_row
    ]
    (gin,) = together([e[1:] for e in ends])
    grad_inputs = trade(join_row([e[0] for e in ends]))
    got_one, got_two, passed_m = lax.optimization_barrier((got_one, got_two, passed_m, ends))[:3]
    sent_one = chip_send(da_one, got_one, n_dp, *one_way)
    sent_two = chip_send(da_two, got_two, n_dp, *two_way)
    passed_one = chip_pass(da_one, got_one, sent_one, n_dp, *one_way)
    passed_two = chip_pass(da_two, got_two, sent_two, n_dp, *two_way)

    def shard_sum(summed):
        return jnp.sum(trade(turn(summed.astype(BF), -tensor)).astype(F32), axis=0)

    sums_m = jnp.concatenate([chip_sum(passed) for passed in passed_m], axis=1)
    sums_a = jnp.concatenate([chip_sum(passed_one), chip_sum(passed_two)])[:, 0]
    gbs = jnp.concatenate([gb_one, gb_two])

    each = width // (n_dp * n_t)
    vectors = jnp.concatenate([gin[0:2], gvec[0:4]])
    vectors = vectors.reshape(6, n_dp, n_t, each).transpose(1, 2, 0, 3).reshape(n_dp, n_t, 6 * each)
    shard = jnp.concatenate(
        [
            gbs.reshape(n_t, 2, n_dp, part // n_dp).transpose(2, 0, 1, 3).reshape(n_dp, n_t, -1),
            gbup.reshape(n_t, n_dp, ff // n_dp).transpose(1, 0, 2),
        ],
        axis=2,
    )
    both = jnp.concatenate([vectors, jnp.roll(shard, tensor, axis=1)], axis=2)
    if n_dp == 8:
        for mask in (1, 2, 4):
            bit = (dp // mask) % 2
            split = both.reshape((both.shape[0] // 2, 2) + both.shape[1:])
            kept = lax.dynamic_index_in_dim(split, bit, 1, keepdims=False)
            sent = lax.dynamic_index_in_dim(split, 1 - bit, 1, keepdims=False)
            both = kept + swap(sent, n_dp, mask)
        both = both[0]
    else:
        both = lax.psum_scatter(both, "dp", scatter_dimension=0, tiled=False)
    parts = turn(jnp.concatenate([p[:, None] for p in in_parts(both)], axis=1), tensor)
    parts = jnp.pad(parts, ((0, 0), (0, 13), (0, width - parts.shape[2])))
    share = shard_sum(after(jnp.concatenate([sums_a.astype(BF), sums_m.astype(BF), parts], axis=1), grad_inputs))
    share_a, share_up, share_down = (share[i * rows : (i + 1) * rows] for i in range(3))
    mine = jnp.sum(share[3 * rows : 3 * rows + 3, 0 : both.shape[1]], axis=0)
    vec_out = mine[0 : 6 * each].reshape(6, each)
    share_b_qv = mine[6 * each : 6 * each + 2 * (part // n_dp)].reshape(2, part // n_dp)
    share_b_up = mine[6 * each + 2 * (part // n_dp) :]
    share_w_qkv = share_a[:, 0 : 3 * part].reshape(rows, 3, part)
    share_w_out = share_a[:, 3 * part :].T
    return (
        block_out,
        grad_inputs,
        vec_out[0],
        vec_out[1],
        share_w_qkv,
        share_b_qv,
        share_w_out,
        vec_out[2],
        vec_out[3],
        vec_out[4],
        share_up,
        share_b_up,
        share_down.T,
        vec_out[5],
    )


def solution(mesh):
    return jax.shard_map(
        functools.partial(local, mesh.shape["dp"], mesh.shape["tensor"]),
        mesh=mesh,
        in_specs=(
            P("dp", "tensor", None),
            P("dp", None),
            P(),
            P(),
            P(None, None, "tensor"),
            P(None, "tensor"),
            P("tensor", None),
            P(),
            P(),
            P(),
            P(None, "tensor"),
            P("tensor"),
            P("tensor", None),
            P(),
            P("dp", "tensor", None),
        ),
        out_specs=(
            P("dp", "tensor", None),
            P("dp", "tensor", None),
            P(("dp", "tensor")),
            P(("dp", "tensor")),
            P("dp", None, "tensor"),
            P(None, ("tensor", "dp")),
            P("tensor", "dp"),
            P(("dp", "tensor")),
            P(("dp", "tensor")),
            P(("dp", "tensor")),
            P("dp", "tensor"),
            P(("tensor", "dp")),
            P("tensor", "dp"),
            P(("dp", "tensor")),
        ),
        check_vma=False,
    )
```

time: 1350 us -> 426 us (0.32)
  waiting for transfers between devices: 892 us -> 75.5 us
  matrix products: 241 us -> 0 us
  Pallas kernels: 0 us -> 141 us
  other arithmetic: 113 us -> 21.5 us
  starting transfers between devices: 0.49 us -> 39.5 us
  blocking collectives: 61.8 us -> 94.7 us
  local copies, waits for them, and re-layouts: 17.5 us -> 44.4 us
  between operations: 16.8 us -> 1.58 us
    all_gather x4 -> x0, waiting for transfers between devices: 449 us -> none  [the longest x1 116 us: local(): resid_rows = lax.all_gather(grad_mixed_low, 'tensor', axis=1, tiled=True)]
    reduce_scatter x7 -> x0, waiting for transfers between devices: 442 us -> none  [the longest x1 109 us: local(): lax.psum_scatter(norm_two_part.astype(jnp.bfloat16), 'tensor', scatter_di...]
    dot_general x24 -> x0, matrix products: 241 us -> none  [the longest x2 32.2 us: attend_backward(): jnp.einsum('rqhe,rkhe->rhqk', grad_blk, value_h, preferred_element_type=j...]
    pallas_call x0 -> x7, Pallas kernels: none -> 141 us  [call(): pl.pallas_call(kernel, grid=grid, out_shape=shapes, in_specs=specs, out_s...]
    all_to_all x0 -> x2, blocking collectives: none -> 94.7 us  [trade(): return lax.all_to_all(value, 'tensor', 0, 0, tiled=True)]
    unnamed x2 -> x0, blocking collectives: 61.8 us -> none
    convert_element_type x8 -> x7, other arithmetic: 58.2 us -> 2.65 us  [the longest x2 1.18 us: chip_pass(): there = (there + sent[1].astype(F32)).astype(BF)]
    reduce_sum x11 -> x2, other arithmetic: 45.7 us -> 0.29 us  [the longest x1 0.27 us: shard_sum(): return jnp.sum(trade(turn(summed.astype(BF), -tensor)).astype(F32), axis=0)]
  transfers between devices with their start and end apart: 12 -> 34, of which waited for: 11 -> 8; matrix products, arithmetic and copies ran while one was open for 11% -> 9% of each run, Pallas kernels for 0% -> 22%
where the time goes in v2:
time: 426 us; the launch traced here: 418 us
  Pallas kernels  141 us (33%)
  blocking collectives  94.7 us (22%)
  waiting for transfers between devices  75.5 us (18%)
  local copies, waits for them, and re-layouts  44.4 us (10%)
  starting transfers between devices  39.5 us (9%)
  other arithmetic  21.5 us (5%)
    pallas_call x7, Pallas kernels, call(): pl.pallas_call(kernel, grid=grid, out_shape=shapes, in_specs=specs, out_s...  141 us
    all_to_all x2, blocking collectives, trade(): return lax.all_to_all(value, 'tensor', 0, 0, tiled=True)  94.7 us
    all_to_all x4, waiting for transfers between devices, trade(): return lax.all_to_all(value, 'tensor', 0, 0, tiled=True)  40 us
    ppermute x30, waiting for transfers between devices, swap(): return lax.ppermute(value, 'dp', [(i, i ^ mask) for i in range(n_dp)])  35.5 us
    ppermute x30, starting transfers between devices, swap(): return lax.ppermute(value, 'dp', [(i, i ^ mask) for i in range(n_dp)])  22.2 us
    all_to_all x4, starting transfers between devices, trade(): return lax.all_to_all(value, 'tensor', 0, 0, tiled=True)  17.3 us
    unnamed x60, local copies, waits for them, and re-layouts  9.29 us
  transfers between devices with their start and end apart: 34, of which 8 were waited for; matrix products, arithmetic and copies ran while one was open for 9% of the time, Pallas kernels for 22%

profile of v2, /device:TPU:0, one launch (start us, length us, event | category | flops | bytes accessed | tf_op | source)
XLA Modules:
  0.0 418.1 jit_solution(11390254528500319577)
XLA Ops:
  5.3 49.4 %all_to_all.30 = bf16[4,304,768]{2,1,0:T(8,128)(2,1)S(1)} all-to-all(bf16[4,304,768]{2,1,0:T(8,128)(2,1)S(1)} %broadcast_in_dim.90), channel_id=1, replica_groups=mesh['dp'=8,'tensor'=4] {'tensor'}, dimensions={0} | all-to-all | bytes 3735552 | tf_op jit(solution)/shard_map/all_to_all | solution.py:462
  54.7 3.6 all-to-all-start.1
  59.4 1.5 collective-permute-start
  60.9 1.5 collective-permute-start.1
  62.9 31.7 %all-to-all-done.1 = bf16[4,256,768]{2,1,0:T(8,128)(2,1)S(1)} async-done(((bf16[4,256,768]{2,1,0:T(8,128)(2,1)}), bf16[4,256,768]{2,1,0:T(8,128)(2,1)S(1)}, u32[]{:S(2)}, u32[]{:S(2)}) %all-to-all-start.1) | async-done | bytes 1572896 | tf_op jit(solution)/shard_map/all_to_all | solution.py:462
  94.6 1.1 copy-done.2
  95.8 4.4 %all-to-all-start.2 = ((bf16[4,256,768]{2,1,0:T(8,128)(2,1)}), bf16[4,256,768]{2,1,0:T(8,128)(2,1)}, u32[]{:S(2)}, u32[]{:S(2)}) async-start(bf16[4,256,768]{2,1,0:T(8,128)(2,1)} %param.30), calls=%async_computation.2 | async-start | bytes 3145728 | tf_op jit(solution)/shard_map/all_to_all | solution.py:462
  101.5 1.5 collective-permute-start.7
  103.0 1.5 collective-permute-start.8
  104.5 1.3 broadcast_in_dim.91.gain_ref
  105.8 1.3 broadcast_in_dim.92.bias_ref
  107.1 2.1 pad_maximum_fusion.own_ref
  110.2 12.1 %collective-permute-done.7 = bf16[3,2,96,768]{3,2,0,1:T(8,128)(2,1)S(1)} collective-permute-done((bf16[3,2,96,768]{3,2,0,1:T(8,128)(2,1)}, bf16[3,2,96,768]{3,2,0,1:T(8,128)(2,1)S(1)}, u32[]{:S(2)}, u32[]{:S(2)}) %collective-permute-start.7) | collective-permute-done | bytes 884768 | tf_op jit(solution)/shard_map/ppermute | solution.py:470
  123.5 1.5 collective-permute-start.10
  128.3 4.3 %first.1.n1t_ref = bf16[768,1024]{1,0:T(8,128)(2,1)} custom-call(f32[1,768]{1,0:T(1,128)} %broadcast_in_dim.91.gain_ref, f32[1,768]{1,0:T(1,128)} %broadcast_in_dim.92.bias_ref, bf16[1024,768]{1,0:T(8,128)(2,1)} %bitcast.152), custom_call_target="tpu_custom_call" | custom-call | flops 1 | bytes 1 | tf_op jit(solution)/shard_map/first/pallas_call | solution.py:58
  133.7 17.4 %attend.2 = (bf16[2,576,1024]{2,1,0:T(8,128)(2,1)}, bf16[2,192,1024]{2,1,0:T(8,128)(2,1)}, f32[2,8,1024]{2,1,0:T(8,128)}, bf16[2,768,768]{2,1,0:T(8,128)(2,1)}) custom-call(s32[8]{0:T(128)} %broadcast_xor_fusion.ids_ref, bf16[768,1024]{1,0:T(8,128)(2,1)} %first.1.n1t_ref, f32[4,3,768]{2,1,0:T(4,128)} %slice_add_fusion.small_ref, ...), custom_call_target="tpu_custom_call" | custom-call | flops 1 | bytes 1 | tf_op jit(solution)/shard_map/attend/pallas_call | solution.py:58
  154.7 17.7 %attend.3 = (bf16[2,576,1024]{2,1,0:T(8,128)(2,1)}, bf16[2,192,1024]{2,1,0:T(8,128)(2,1)}, f32[2,8,1024]{2,1,0:T(8,128)}, bf16[2,768,768]{2,1,0:T(8,128)(2,1)}) custom-call(s32[8]{0:T(128)} %broadcast_xor_fusion.ids_ref, bf16[768,1024]{1,0:T(8,128)(2,1)} %first.1.n1t_ref, f32[4,3,768]{2,1,0:T(4,128)} %slice_add_fusion.small_ref, ...), custom_call_target="tpu_custom_call" | custom-call | flops 1 | bytes 1 | tf_op jit(solution)/shard_map/attend/pallas_call | solution.py:58
  176.1 2.1 copy.149.refs_7_
  178.2 47.9 %mlp.1 = (bf16[1024,768]{1,0:T(8,128)(2,1)}, f32[1024,768]{1,0:T(8,128)}, bf16[768,1024]{1,0:T(8,128)(2,1)}, f32[8,768]{1,0:T(8,128)}, f32[4,1,768]{2,1,0:T(1,12...) custom-call(s32[8]{0:T(128)} %broadcast_xor_fusion.ids_ref, bf16[1024,768]{1,0:T(8,128)(2,1)} %bitcast.153, ...), custom_call_target="tpu_custom_call" | custom-call | flops 1 | bytes 1 | tf_op jit(solution)/shard_map/mlp/pallas_call | solution.py:58
  226.1 4.9 %copy.151 = bf16[4,4,2,96,768]{4,3,1,2,0:T(8,128)(2,1)} copy(bf16[4,4,2,96,768]{4,3,2,1,0:T(8,128)(2,1)} %get-tuple-element.109) | data formatting | bytes 9437184 | tf_op jit(solution)/shard_map/mlp/pallas_call | solution.py:58
  231.5 21.7 %attend_back.2 = (bf16[2,576,1024]{2,1,0:T(8,128)(2,1)}, f32[2,2,192]{2,1,0:T(2,128)}, bf16[4,2,1,96,768]{4,3,2,1,0:T(8,128)(2,1)}, bf16[4,2,1,96,768]{4,3,2,1,0:T(8,128)(2,1)}) custom-call(s32[8]{0:T(128)} %broadcast_xor_fusion.ids_ref, bf16[768,1024]{1,0:T(8,128)(2,1)} %get-tuple-element.116.gmt_ref, bf16[768,1024]{1,0:T(8,128)(2,1)} %first.1.n1t_ref, ...), custom_call_target="tpu_custom_call" | custom-call | flops 1 | bytes 1 | tf_op jit(solution)/shard_map/attend_back/pallas_call | solution.py:58
  253.2 4.9 %all-to-all-start.3 = ((bf16[4,256,768]{2,1,0:T(8,128)(2,1)}), bf16[4,256,768]{2,1,0:T(8,128)(2,1)S(1)}, u32[]{:S(2)}, u32[]{:S(2)}) async-start(bf16[4,256,768]{2,1,0:T(8,128)(2,1)} %bitcast.42), calls=%async_computation.3 | async-start | bytes 3145728 | tf_op jit(solution)/shard_map/all_to_all | solution.py:462
  258.2 2.3 slice_bitcast_fusion.3
  260.4 2.2 slice_bitcast_fusion.9
  263.1 1.1 pad_maximum_fusion.2
  264.9 1.1 pad_maximum_fusion.1
  267.1 21.2 %attend_back.3 = (bf16[2,576,1024]{2,1,0:T(8,128)(2,1)}, f32[2,2,192]{2,1,0:T(2,128)}, bf16[4,2,1,96,768]{4,3,2,1,0:T(8,128)(2,1)}, bf16[4,2,1,96,768]{4,3,2,1,0:T(8,128)(2,1)}) custom-call(s32[8]{0:T(128)} %broadcast_xor_fusion.ids_ref, bf16[768,1024]{1,0:T(8,128)(2,1)} %get-tuple-element.116.gmt_ref, bf16[768,1024]{1,0:T(8,128)(2,1)} %first.1.n1t_ref, ...), custom_call_target="tpu_custom_call" | custom-call | flops 1 | bytes 1 | tf_op jit(solution)/shard_map/attend_back/pallas_call | solution.py:58
  289.4 6.3 %all-to-all-done.3 = bf16[4,256,768]{2,1,0:T(8,128)(2,1)S(1)} async-done(((bf16[4,256,768]{2,1,0:T(8,128)(2,1)}), bf16[4,256,768]{2,1,0:T(8,128)(2,1)S(1)}, u32[]{:S(2)}, u32[]{:S(2)}) %all-to-all-start.3) | async-done | bytes 1572896 | tf_op jit(solution)/shard_map/all_to_all | solution.py:462
  295.7 3.6 slice_bitcast_fusion
  299.4 10.7 %input_back.1 = (bf16[1024,768]{1,0:T(8,128)(2,1)}, f32[8,768]{1,0:T(8,128)}) custom-call(bf16[1024,768]{1,0:T(8,128)(2,1)} %bitcast.154, f32[1024,768]{1,0:T(8,128)} %get-tuple-element.122.gm_ref, f32[1,768]{1,0:T(1,128)} %broadcast_in_dim.91.gain_ref, bf16[2,768,768]{2,1,0:T(8,128)(2,1)} %get-tuple-element.86.out_two_ref.a_ref.a_one_ref, ...), custom_call_target="tpu_custom_call" | custom-call | flops 1 | bytes 1 | tf_op jit(solution)/shard_map/input_back/pallas_call | solution.py:58
  311.4 2.4 slice_bitcast_fusion.6
  314.8 3.9 convert_add_fusion.1
  320.4 1.6 collective-permute-start.29
  322.0 4.5 %all-to-all-start.4 = ((bf16[4,256,768]{2,1,0:T(8,128)(2,1)}), bf16[4,256,768]{2,1,0:T(8,128)(2,1)}, u32[]{:S(2)}, u32[]{:S(2)}) async-start(bf16[4,256,768]{2,1,0:T(8,128)(2,1)} %bitcast.168), calls=%async_computation.4 | async-start | bytes 3145728 | tf_op jit(solution)/shard_map/all_to_all | solution.py:462
  326.5 8.0 %collective-permute-done.29 = f32[1,4,288]{2,0,1:T(1,128)S(1)} collective-permute-done((f32[1,4,288]{2,0,1:T(1,128)S(1)}, f32[1,4,288]{2,0,1:T(1,128)S(1)}, u32[]{:S(2)}, u32[]{:S(2)}) %collective-permute-start.29) | collective-permute-done | bytes 4640 | tf_op jit(solution)/shard_map/ppermute | solution.py:470
  335.3 1.3 add_convert_fusion.10
  336.7 1.2 collective-permute-start.23
  338.1 1.6 collective-permute-start.25
  339.8 1.2 add_convert_fusion.1
  341.0 10.4 %collective-permute-done.23 = bf16[2,2,1,96,768]{4,3,1,2,0:T(8,128)(2,1)S(1)} collective-permute-done((bf16[2,2,1,96,768]{4,3,1,2,0:T(8,128)(2,1)S(1)}, bf16[2,2,1,96,768]{4,3,1,2,0:T(8,128)(2,1)S(1)}, u32[]{:S(2)}, u32[]{:S(2)}) %collective-permute-start.23) | collective-permute-done | bytes 589856 | tf_op jit(solution)/shard_map/ppermute | solution.py:470
  352.4 1.3 collective-permute-start.24
  353.8 1.2 collective-permute-start.26
  355.1 4.7 %collective-permute-done.24 = bf16[2,1,96,768]{3,2,0,1:T(8,128)(2,1)S(1)} collective-permute-done((bf16[2,1,96,768]{3,2,0,1:T(8,128)(2,1)S(1)}, bf16[2,1,96,768]{3,2,0,1:T(8,128)(2,1)S(1)}, u32[]{:S(2)}, u32[]{:S(2)}) %collective-permute-start.24) | collective-permute-done | bytes 294944 | tf_op jit(solution)/shard_map/ppermute | solution.py:470
  359.8 1.1 fusion.12
  361.2 1.9 all-to-all-done.4
  363.8 45.3 %all_to_all.31 = bf16[4,304,768]{2,1,0:T(8,128)(2,1)S(1)} all-to-all(bf16[4,304,768]{2,1,0:T(8,128)(2,1)S(1)} %fusion.2), channel_id=1, replica_groups=mesh['dp'=8,'tensor'=4] {'tensor'}, dimensions={0} | all-to-all | bytes 3735552 | tf_op jit(solution)/shard_map/all_to_all | solution.py:462
  414.0 1.1 copy.190
  415.2 2.7 copy.191
  (179 shorter events, 37.4 us)
Async XLA Ops:
  0.6 126.3 %copy-start = (s32[4,1024]{1,0:T(4,128)S(1)}, s32[4,1024]{1,0:T(4,128)}, u32[]{:S(2)}) copy-start(s32[4,1024]{1,0:T(4,128)} %param.17) | copy-start | bytes 49156
  54.7 8.2 %copy-start.4 = (bf16[4,304,768]{2,1,0:T(8,128)(2,1)}, bf16[4,304,768]{2,1,0:T(8,128)(2,1)S(1)}, u32[]{:S(2)}) copy-start(bf16[4,304,768]{2,1,0:T(8,128)(2,1)S(1)} %all_to_all.30) | copy-start | bytes 5603332
  54.7 39.9 %all-to-all-start.1 = ((bf16[4,256,768]{2,1,0:T(8,128)(2,1)}), bf16[4,256,768]{2,1,0:T(8,128)(2,1)S(1)}, u32[]{:S(2)}, u32[]{:S(2)}) async-start(bf16[4,256,768]{2,1,0:T(8,128)(2,1)} %param.16), calls=%async_computation.1 | async-start | bytes 3145728 | tf_op jit(solution)/shard_map/all_to_all | solution.py:462
  59.4 41.1 %collective-permute-start = (bf16[3,1,96,768]{3,2,0,1:T(8,128)(2,1)}, bf16[3,1,96,768]{3,2,0,1:T(8,128)(2,1)}, u32[]{:S(2)}, u32[]{:S(2)}) collective-permute-start(bf16[3,1,96,768]{3,2,0,1:T(8,128)(2,1)} %get-tuple-element.210), channel_id=1, source_target_pairs={{0,8},{4,12},{8,0},{12,4},{16,24},{20,28},{24,16},{28,20},{1,9},{5... | collective-permute-start | bytes 1327112 | tf_op jit(solution)/shard_map/ppermute | solution.py:470
  60.9 39.6 %collective-permute-start.1 = (bf16[3,1,96,768]{3,2,0,1:T(8,128)(2,1)}, bf16[3,1,96,768]{3,2,0,1:T(8,128)(2,1)}, u32[]{:S(2)}, u32[]{:S(2)}) collective-permute-start(bf16[3,1,96,768]{3,2,0,1:T(8,128)(2,1)} %get-tuple-element.210), channel_id=1, source_target_pairs={{0,16},{4,20},{8,24},{12,28},{16,0},{20,4},{24,8},{28,12},{1,17},{... | collective-permute-start | bytes 1327112 | tf_op jit(solution)/shard_map/ppermute | solution.py:470
  62.5 38.1 %collective-permute-start.2 = (bf16[3,1,96,768]{3,2,0,1:T(8,128)(2,1)}, bf16[3,1,96,768]{3,2,0,1:T(8,128)(2,1)}, u32[]{:S(2)}, u32[]{:S(2)}) collective-permute-start(bf16[3,1,96,768]{3,2,0,1:T(8,128)(2,1)} %get-tuple-element.210), channel_id=1, source_target_pairs={{0,24},{4,28},{8,16},{12,20},{16,8},{20,12},{24,0},{28,4},{1,25},{... | collective-permute-start | bytes 1327112 | tf_op jit(solution)/shard_map/ppermute | solution.py:470
  95.8 77.3 %all-to-all-start.2 = ((bf16[4,256,768]{2,1,0:T(8,128)(2,1)}), bf16[4,256,768]{2,1,0:T(8,128)(2,1)}, u32[]{:S(2)}, u32[]{:S(2)}) async-start(bf16[4,256,768]{2,1,0:T(8,128)(2,1)} %param.30), calls=%async_computation.2 | async-start | bytes 3145728 | tf_op jit(solution)/shard_map/all_to_all | solution.py:462
  100.5 50.6 %copy-start.3 = (bf16[3,192,768]{2,1,0:T(8,128)(2,1)}, bf16[3,192,768]{2,1,0:T(8,128)(2,1)S(1)}, u32[]{:S(2)}) copy-start(bf16[3,192,768]{2,1,0:T(8,128)(2,1)S(1)} %fusion.5) | copy-start | bytes 2654212
  100.5 6.6 %copy-start.7 = (bf16[768,3,192]{0,2,1:T(8,128)(2,1)S(1)}, bf16[768,3,192]{0,2,1:T(8,128)(2,1)}, u32[]{:S(2)}) copy-start(bf16[768,3,192]{0,2,1:T(8,128)(2,1)} %param.20) | copy-start | bytes 2654212
  101.5 20.8 %collective-permute-start.7 = (bf16[3,2,96,768]{3,2,0,1:T(8,128)(2,1)}, bf16[3,2,96,768]{3,2,0,1:T(8,128)(2,1)S(1)}, u32[]{:S(2)}, u32[]{:S(2)}) collective-permute-start(bf16[3,2,96,768]{3,2,0,1:T(8,128)(2,1)} %copy.134), channel_id=1, source_target_pairs={{0,8},{4,12},{8,0},{12,4},{16,24},{20,28},{24,16},{28,20},{1,9},{5... | collective-permute-start | bytes 2654216 | tf_op jit(solution)/shard_map/ppermute | solution.py:470
  103.0 20.5 %collective-permute-start.8 = (bf16[3,2,96,768]{3,2,0,1:T(8,128)(2,1)}, bf16[3,2,96,768]{3,2,0,1:T(8,128)(2,1)S(1)}, u32[]{:S(2)}, u32[]{:S(2)}) collective-permute-start(bf16[3,2,96,768]{3,2,0,1:T(8,128)(2,1)} %copy.134), channel_id=1, source_target_pairs={{0,16},{4,20},{8,24},{12,28},{16,0},{20,4},{24,8},{28,12},{1,17},{... | collective-permute-start | bytes 2654216 | tf_op jit(solution)/shard_map/ppermute | solution.py:470
  104.5 21.4 %collective-permute-start.3 = (bf16[3,1,96,768]{3,2,0,1:T(8,128)(2,1)}, bf16[3,1,96,768]{3,2,0,1:T(8,128)(2,1)}, u32[]{:S(2)}, u32[]{:S(2)}) collective-permute-start(bf16[3,1,96,768]{3,2,0,1:T(8,128)(2,1)} %get-tuple-element.210), channel_id=1, source_target_pairs={{0,4},{4,0},{8,12},{12,8},{16,20},{20,16},{24,28},{28,24},{1,5},{5... | collective-permute-start | bytes 1327112 | tf_op jit(solution)/shard_map/ppermute | solution.py:470
  109.2 18.4 %slice-start.1 = ((bf16[4,304,768]{2,1,0:T(8,128)(2,1)}), bf16[4,16,768]{2,1,0:T(8,128)(2,1)S(1)}, s32[]{:S(2)}) async-start(bf16[4,304,768]{2,1,0:T(8,128)(2,1)} %copy-done.4), calls=%async_computation.7 | async-start | bytes 196608 | tf_op jit(solution)/shard_map/slice | solution.py:571
  109.7 22.8 %collective-permute-start.4 = (bf16[3,1,96,768]{3,2,0,1:T(8,128)(2,1)}, bf16[3,1,96,768]{3,2,0,1:T(8,128)(2,1)S(1)}, u32[]{:S(2)}, u32[]{:S(2)}) collective-permute-start(bf16[3,1,96,768]{3,2,0,1:T(8,128)(2,1)} %collective-permute-done), channel_id=1, source_target_pairs={{0,4},{4,0},{8,12},{12,8},{16,20},{20,16},{24,28},{28,24},{1,5},{5... | collective-permute-start | bytes 1327112 | tf_op jit(solution)/shard_map/ppermute | solution.py:470
  110.2 22.3 %collective-permute-start.5 = (bf16[3,1,96,768]{3,2,0,1:T(8,128)(2,1)}, bf16[3,1,96,768]{3,2,0,1:T(8,128)(2,1)S(1)}, u32[]{:S(2)}, u32[]{:S(2)}) collective-permute-start(bf16[3,1,96,768]{3,2,0,1:T(8,128)(2,1)} %collective-permute-done.1), channel_id=1, source_target_pairs={{0,4},{4,0},{8,12},{12,8},{16,20},{20,16},{24,28},{28,24},{1,5},{5... | collective-permute-start | bytes 1327112 | tf_op jit(solution)/shard_map/ppermute | solution.py:470
  122.3 10.3 %collective-permute-start.6 = (bf16[3,1,96,768]{3,2,0,1:T(8,128)(2,1)}, bf16[3,1,96,768]{3,2,0,1:T(8,128)(2,1)S(1)}, u32[]{:S(2)}, u32[]{:S(2)}) collective-permute-start(bf16[3,1,96,768]{3,2,0,1:T(8,128)(2,1)} %collective-permute-done.2), channel_id=1, source_target_pairs={{0,4},{4,0},{8,12},{12,8},{16,20},{20,16},{24,28},{28,24},{1,5},{5... | collective-permute-start | bytes 1327112 | tf_op jit(solution)/shard_map/ppermute | solution.py:470
  123.5 27.6 %collective-permute-start.10 = (bf16[3,1,96,768]{3,2,0,1:T(8,128)(2,1)}, bf16[3,1,96,768]{3,2,0,1:T(8,128)(2,1)}, u32[]{:S(2)}, u32[]{:S(2)}) collective-permute-start(bf16[3,1,96,768]{3,2,0,1:T(8,128)(2,1)} %slice.343), channel_id=1, source_target_pairs={{0,16},{4,20},{8,24},{12,28},{16,0},{20,4},{24,8},{28,12},{1,17},{... | collective-permute-start | bytes 1327112 | tf_op jit(solution)/shard_map/ppermute | solution.py:470
  125.9 25.2 %collective-permute-start.9 = (bf16[3,1,96,768]{3,2,0,1:T(8,128)(2,1)}, bf16[3,1,96,768]{3,2,0,1:T(8,128)(2,1)}, u32[]{:S(2)}, u32[]{:S(2)}) collective-permute-start(bf16[3,1,96,768]{3,2,0,1:T(8,128)(2,1)} %slice.342), channel_id=1, source_target_pairs={{0,8},{4,12},{8,0},{12,4},{16,24},{20,28},{24,16},{28,20},{1,9},{5... | collective-permute-start | bytes 1327112 | tf_op jit(solution)/shard_map/ppermute | solution.py:470
  133.7 18.6 %copy-start.22 = (f32[768]{0:T(1024)S(1)}, f32[768]{0:T(1024)}, u32[]{:S(2)}) copy-start(f32[768]{0:T(1024)} %param.23) | copy-start | bytes 9220
  133.7 19.2 %copy-start.23 = (f32[768]{0:T(1024)S(1)}, f32[768]{0:T(1024)}, u32[]{:S(2)}) copy-start(f32[768]{0:T(1024)} %param.24) | copy-start | bytes 9220
  133.7 19.8 %copy-start.24 = (f32[768]{0:T(1024)S(1)}, f32[768]{0:T(1024)}, u32[]{:S(2)}) copy-start(f32[768]{0:T(1024)} %param.25) | copy-start | bytes 9220
  133.7 20.4 %copy-start.25 = (f32[768]{0:T(1024)S(1)}, f32[768]{0:T(1024)}, u32[]{:S(2)}) copy-start(f32[768]{0:T(1024)} %param.29) | copy-start | bytes 9220
  151.1 21.3 %collective-permute-start.11 = (bf16[3,2,96,768]{3,2,1,0:T(8,128)(2,1)S(1)}, bf16[3,2,96,768]{3,2,1,0:T(8,128)(2,1)}, u32[]{:S(2)}, u32[]{:S(2)}) collective-permute-start(bf16[3,2,96,768]{3,2,1,0:T(8,128)(2,1)S(1)} %bitcast.156), channel_id=1, source_target_pairs={{0,4},{4,0},{8,12},{12,8},{16,20},{20,16},{24,28},{28,24},{1,5},{5... | collective-permute-start | bytes 2654216 | tf_op jit(solution)/shard_map/ppermute | solution.py:470
  151.2 21.2 %collective-permute-start.12 = (bf16[3,2,96,768]{3,2,0,1:T(8,128)(2,1)S(1)}, bf16[3,2,96,768]{3,2,0,1:T(8,128)(2,1)S(1)}, u32[]{:S(2)}, u32[]{:S(2)}) collective-permute-start(bf16[3,2,96,768]{3,2,0,1:T(8,128)(2,1)S(1)} %collective-permute-done.7), channel_id=1, source_target_pairs={{0,4},{4,0},{8,12},{12,8},{16,20},{20,16},{24,28},{28,24},{1,5},{5... | collective-permute-start | bytes 2654216 | tf_op jit(solution)/shard_map/ppermute | solution.py:470
  151.7 21.4 %collective-permute-start.13 = (bf16[3,2,96,768]{3,2,0,1:T(8,128)(2,1)S(1)}, bf16[3,2,96,768]{3,2,0,1:T(8,128)(2,1)}, u32[]{:S(2)}, u32[]{:S(2)}) collective-permute-start(bf16[3,2,96,768]{3,2,0,1:T(8,128)(2,1)S(1)} %collective-permute-done.8), channel_id=1, source_target_pairs={{0,4},{4,0},{8,12},{12,8},{16,20},{20,16},{24,28},{28,24},{1,5},{5... | collective-permute-start | bytes 2654216 | tf_op jit(solution)/shard_map/ppermute | solution.py:470
  151.8 20.6 %collective-permute-start.14 = (bf16[3,1,96,768]{3,2,0,1:T(8,128)(2,1)}, bf16[3,1,96,768]{3,2,0,1:T(8,128)(2,1)S(1)}, u32[]{:S(2)}, u32[]{:S(2)}) collective-permute-start(bf16[3,1,96,768]{3,2,0,1:T(8,128)(2,1)} %collective-permute-done.9), channel_id=1, source_target_pairs={{0,4},{4,0},{8,12},{12,8},{16,20},{20,16},{24,28},{28,24},{1,5},{5... | collective-permute-start | bytes 1327112 | tf_op jit(solution)/shard_map/ppermute | solution.py:470
  152.2 20.2 %collective-permute-start.15 = (bf16[3,1,96,768]{3,2,0,1:T(8,128)(2,1)}, bf16[3,1,96,768]{3,2,0,1:T(8,128)(2,1)}, u32[]{:S(2)}, u32[]{:S(2)}) collective-permute-start(bf16[3,1,96,768]{3,2,0,1:T(8,128)(2,1)} %collective-permute-done.10), channel_id=1, source_target_pairs={{0,4},{4,0},{8,12},{12,8},{16,20},{20,16},{24,28},{28,24},{1,5},{5... | collective-permute-start | bytes 1327112 | tf_op jit(solution)/shard_map/ppermute | solution.py:470
  231.0 27.1 %collective-permute-start.17 = (bf16[4,4,2,96,768]{4,3,1,2,0:T(8,128)(2,1)}, bf16[4,4,2,96,768]{4,3,1,2,0:T(8,128)(2,1)}, u32[]{:S(2)}, u32[]{:S(2)}) collective-permute-start(bf16[4,4,2,96,768]{4,3,1,2,0:T(8,128)(2,1)} %copy.151), channel_id=1, source_target_pairs={{0,4},{4,0},{8,12},{12,8},{16,20},{20,16},{24,28},{28,24},{1,5},{5... | collective-permute-start | bytes 14155784 | tf_op jit(solution)/shard_map/ppermute | solution.py:470
  253.1 36.2 %collective-permute-start.16 = (bf16[4,2,1,96,768]{4,3,1,2,0:T(8,128)(2,1)}, bf16[4,2,1,96,768]{4,3,1,2,0:T(8,128)(2,1)S(1)}, u32[]{:S(2)}, u32[]{:S(2)}) collective-permute-start(bf16[4,2,1,96,768]{4,3,1,2,0:T(8,128)(2,1)} %bitcast.184), channel_id=1, source_target_pairs={{0,4},{4,0},{8,12},{12,8},{16,20},{20,16},{24,28},{28,24},{1,5},{5... | collective-permute-start | bytes 3538952 | tf_op jit(solution)/shard_map/ppermute | solution.py:470
  253.2 42.5 %all-to-all-start.3 = ((bf16[4,256,768]{2,1,0:T(8,128)(2,1)}), bf16[4,256,768]{2,1,0:T(8,128)(2,1)S(1)}, u32[]{:S(2)}, u32[]{:S(2)}) async-start(bf16[4,256,768]{2,1,0:T(8,128)(2,1)} %bitcast.42), calls=%async_computation.3 | async-start | bytes 3145728 | tf_op jit(solution)/shard_map/all_to_all | solution.py:462
  264.2 31.5 %collective-permute-start.19 = (bf16[2,4,96,768]{3,2,1,0:T(8,128)(2,1)}, bf16[2,4,96,768]{3,2,1,0:T(8,128)(2,1)}, u32[]{:S(2)}, u32[]{:S(2)}) collective-permute-start(bf16[2,4,96,768]{3,2,1,0:T(8,128)(2,1)} %pad_maximum_fusion.2), channel_id=1, source_target_pairs={{0,16},{4,20},{8,24},{12,28},{16,0},{20,4},{24,8},{28,12},{1,17},{... | collective-permute-start | bytes 3538952 | tf_op jit(solution)/shard_map/ppermute | solution.py:470
  266.0 29.7 %collective-permute-start.18 = (bf16[2,4,96,768]{3,2,1,0:T(8,128)(2,1)}, bf16[2,4,96,768]{3,2,1,0:T(8,128)(2,1)}, u32[]{:S(2)}, u32[]{:S(2)}) collective-permute-start(bf16[2,4,96,768]{3,2,1,0:T(8,128)(2,1)} %pad_maximum_fusion.1), channel_id=1, source_target_pairs={{0,8},{4,12},{8,0},{12,4},{16,24},{20,28},{24,16},{28,20},{1,9},{5... | collective-permute-start | bytes 3538952 | tf_op jit(solution)/shard_map/ppermute | solution.py:470
  267.1 21.3 %copy-start.26 = (f32[2,2,192]{2,1,0:T(2,128)S(1)}, f32[2,2,192]{2,1,0:T(2,128)}, u32[]{:S(2)}) copy-start(f32[2,2,192]{2,1,0:T(2,128)} %get-tuple-element.139) | copy-start | bytes 9220
  288.3 46.1 %collective-permute-start.20 = (bf16[4,2,1,96,768]{4,3,2,1,0:T(8,128)(2,1)}, bf16[4,2,1,96,768]{4,3,2,1,0:T(8,128)(2,1)}, u32[]{:S(2)}, u32[]{:S(2)}) collective-permute-start(bf16[4,2,1,96,768]{4,3,2,1,0:T(8,128)(2,1)} %get-tuple-element.125), channel_id=1, source_target_pairs={{0,4},{4,0},{8,12},{12,8},{16,20},{20,16},{24,28},{28,24},{1,5},{5... | collective-permute-start | bytes 3538952 | tf_op jit(solution)/shard_map/ppermute | solution.py:470
  289.4 6.3 %copy-start.14 = (bf16[4,2,1,96,768]{4,3,1,2,0:T(8,128)(2,1)}, bf16[4,2,1,96,768]{4,3,1,2,0:T(8,128)(2,1)S(1)}, u32[]{:S(2)}) copy-start(bf16[4,2,1,96,768]{4,3,1,2,0:T(8,128)(2,1)S(1)} %collective-permute-done.16) | copy-start | bytes 3538948
  311.3 2.4 collective-permute-start.27
  313.8 6.5 %collective-permute-start.28 = (f32[2,4,288]{2,0,1:T(2,128)S(1)}, f32[2,4,288]{2,0,1:T(2,128)S(1)}, u32[]{:S(2)}, u32[]{:S(2)}) collective-permute-start(f32[2,4,288]{2,0,1:T(2,128)S(1)} %bitcast.183), channel_id=1, source_target_pairs={{0,8},{4,12},{8,0},{12,4},{16,24},{20,28},{24,16},{28,20},{1,9},{5... | collective-permute-start | bytes 27656 | tf_op jit(solution)/shard_map/ppermute | solution.py:470
  318.7 15.7 %collective-permute-start.21 = (bf16[4,96,768]{2,1,0:T(8,128)(2,1)}, bf16[4,96,768]{2,1,0:T(8,128)(2,1)}, u32[]{:S(2)}, u32[]{:S(2)}) collective-permute-start(bf16[4,96,768]{2,1,0:T(8,128)(2,1)} %get-tuple-element.206), channel_id=1, source_target_pairs={{0,16},{4,20},{8,24},{12,28},{16,0},{20,4},{24,8},{28,12},{1,17},{... | collective-permute-start | bytes 1769480 | tf_op jit(solution)/shard_map/ppermute | solution.py:470
  319.2 15.2 %collective-permute-start.22 = (bf16[4,96,768]{2,1,0:T(8,128)(2,1)}, bf16[4,96,768]{2,1,0:T(8,128)(2,1)S(1)}, u32[]{:S(2)}, u32[]{:S(2)}) collective-permute-start(bf16[4,96,768]{2,1,0:T(8,128)(2,1)} %get-tuple-element.207), channel_id=1, source_target_pairs={{0,8},{4,12},{8,0},{12,4},{16,24},{20,28},{24,16},{28,20},{1,9},{5... | collective-permute-start | bytes 1769480 | tf_op jit(solution)/shard_map/ppermute | solution.py:470
  320.4 14.1 %collective-permute-start.29 = (f32[1,4,288]{2,0,1:T(1,128)S(1)}, f32[1,4,288]{2,0,1:T(1,128)S(1)}, u32[]{:S(2)}, u32[]{:S(2)}) collective-permute-start(f32[1,4,288]{2,0,1:T(1,128)S(1)} %constant_dynamic-slice_fusion), channel_id=1, source_target_pairs={{0,16},{4,20},{8,24},{12,28},{16,0},{20,4},{24,8},{28,12},{1,17},{... | collective-permute-start | bytes 13832 | tf_op jit(solution)/shard_map/ppermute | solution.py:470
  322.0 13.4 %copy-start.16 = (bf16[4,2,1,96,768]{4,3,2,1,0:T(8,128)(2,1)S(1)}, bf16[4,2,1,96,768]{4,3,2,1,0:T(8,128)(2,1)}, u32[]{:S(2)}) copy-start(bf16[4,2,1,96,768]{4,3,2,1,0:T(8,128)(2,1)} %get-tuple-element.124) | copy-start | bytes 3538948
  322.0 41.2 %all-to-all-start.4 = ((bf16[4,256,768]{2,1,0:T(8,128)(2,1)}), bf16[4,256,768]{2,1,0:T(8,128)(2,1)}, u32[]{:S(2)}, u32[]{:S(2)}) async-start(bf16[4,256,768]{2,1,0:T(8,128)(2,1)} %bitcast.168), calls=%async_computation.4 | async-start | bytes 3145728 | tf_op jit(solution)/shard_map/all_to_all | solution.py:462
  336.7 14.6 %collective-permute-start.23 = (bf16[2,2,1,96,768]{4,3,1,2,0:T(8,128)(2,1)S(1)}, bf16[2,2,1,96,768]{4,3,1,2,0:T(8,128)(2,1)S(1)}, u32[]{:S(2)}, u32[]{:S(2)}) collective-permute-start(bf16[2,2,1,96,768]{4,3,1,2,0:T(8,128)(2,1)S(1)} %pad_maximum_fusion.3), channel_id=1, source_target_pairs={{0,8},{4,12},{8,0},{12,4},{16,24},{20,28},{24,16},{28,20},{1,9},{5... | collective-permute-start | bytes 1769480 | tf_op jit(solution)/shard_map/ppermute | solution.py:470
  338.1 15.6 %collective-permute-start.25 = (bf16[2,2,1,96,768]{4,3,1,2,0:T(8,128)(2,1)S(1)}, bf16[2,2,1,96,768]{4,3,1,2,0:T(8,128)(2,1)S(1)}, u32[]{:S(2)}, u32[]{:S(2)}) collective-permute-start(bf16[2,2,1,96,768]{4,3,1,2,0:T(8,128)(2,1)S(1)} %pad_maximum_fusion.4), channel_id=1, source_target_pairs={{0,16},{4,20},{8,24},{12,28},{16,0},{20,4},{24,8},{28,12},{1,17},{... | collective-permute-start | bytes 1769480 | tf_op jit(solution)/shard_map/ppermute | solution.py:470
  341.0 14.0 %copy-start.5 = (f32[4,96,768]{2,1,0:T(8,128)S(1)}, f32[4,96,768]{2,1,0:T(8,128)}, u32[]{:S(2)}) copy-start(f32[4,96,768]{2,1,0:T(8,128)} %get-tuple-element.135) | copy-start | bytes 3538948
  341.0 14.0 %copy-start.18 = (bf16[4,96,768]{2,1,0:T(8,128)(2,1)S(1)}, bf16[4,96,768]{2,1,0:T(8,128)(2,1)}, u32[]{:S(2)}) copy-start(bf16[4,96,768]{2,1,0:T(8,128)(2,1)} %copy-done.17) | copy-start | bytes 1769476
  352.4 7.3 %collective-permute-start.24 = (bf16[2,1,96,768]{3,2,0,1:T(8,128)(2,1)S(1)}, bf16[2,1,96,768]{3,2,0,1:T(8,128)(2,1)S(1)}, u32[]{:S(2)}, u32[]{:S(2)}) collective-permute-start(bf16[2,1,96,768]{3,2,0,1:T(8,128)(2,1)S(1)} %fusion.15), channel_id=1, source_target_pairs={{0,16},{4,20},{8,24},{12,28},{16,0},{20,4},{24,8},{28,12},{1,17},{... | collective-permute-start | bytes 884744 | tf_op jit(solution)/shard_map/ppermute | solution.py:470
  353.8 7.1 %collective-permute-start.26 = (bf16[2,1,96,768]{3,2,0,1:T(8,128)(2,1)S(1)}, bf16[2,1,96,768]{3,2,0,1:T(8,128)(2,1)S(1)}, u32[]{:S(2)}, u32[]{:S(2)}) collective-permute-start(bf16[2,1,96,768]{3,2,0,1:T(8,128)(2,1)S(1)} %fusion.14), channel_id=1, source_target_pairs={{0,8},{4,12},{8,0},{12,4},{16,24},{20,28},{24,16},{28,20},{1,9},{5... | collective-permute-start | bytes 884744 | tf_op jit(solution)/shard_map/ppermute | solution.py:470
  (16 other events, 35.4 us)
